TPU v7x, 256 devices: a whole 4x4x8 slice. The times are simulated.
256 devices in a mesh: span: 16 (over z, core), qry: 16 (over y, x).
Axes of the slice: x: 4, y: 4, z: 8, core: 2. Of those that a mesh axis runs over, the one named last changes fastest.
Arguments:
- features: bfloat16 [16, 32, 128, 256], P('span', 'qry'), may hold values from -6 to 6
- conv_weight: bfloat16 [27, 256, 256], replicated, may hold values from -0.078125 to 0.078125
- queries: float32 [128, 256], P('qry'), may hold values from -600 to 600
- w_query: bfloat16 [2, 256, 256], replicated, may hold values from -0.26171875 to 0.26171875
- w_key: bfloat16 [2, 256, 256], replicated, may hold values from -0.26171875 to 0.26171875
- w_value: bfloat16 [2, 256, 256], replicated, may hold values from -0.26171875 to 0.26171875
- w_out: bfloat16 [2, 256, 256], replicated, may hold values from -0.26171875 to 0.26171875
- norm_gain: float32 [256], replicated, may hold values from 0.5 to 1.5
- mask_weight: bfloat16 [256, 256], replicated, may hold values from -0.375 to 0.375
- mask_blocks: int32 [128, 4], replicated, may hold values from 0 to 511, as said below
Outputs:
- query_embed: float32 [128, 256], P('qry')
- mask_logits: bfloat16 [128, 16, 32, 128], P(None, 'span', 'qry')
Inputs may be any that keep to these rules, and one draw needn't show every extreme that they name: `mask_blocks`: each row lists 4 distinct mask blocks, block z * 32 + y being the voxels pixel[z, y, :]; no block appears twice in the whole array.
All inputs are finite; a program needn't handle non-finite values.
Results may differ from a plain program's by a relative error of at most 0.04.
The roundings to bfloat16 on the way count: a program that leaves them out, or rounds other values in their place, can miss the bound.
Values may be sent and summed in bfloat16 or wider, within the bound.
A program may use at most 64 MiB of HBM per device.

v0:
```python
import math

import jax
import jax.numpy as jnp
from jax import lax
from jax.sharding import PartitionSpec as P

HEADS = 8
LAYERS = 2


def with_halo(cells, sides, width):
    for axis, dim in sides:
        count = lax.axis_size(axis)
        ends = count - 1
        head = lax.slice_in_dim(cells, 0, width, axis=dim)
        tail = lax.slice_in_dim(cells, cells.shape[dim] - width, cells.shape[dim], axis=dim)
        cells = jnp.concatenate(
            [
                lax.ppermute(tail, axis, [(i, (i + 1) % count) for i in range(ends)]),
                cells,
                lax.ppermute(head, axis, [((i + 1) % count, i) for i in range(ends)]),
            ],
            axis=dim,
        )
    return cells


def from_everyone(x, axis):
    size = lax.axis_size(axis)
    return lax.all_to_all(jnp.broadcast_to(x[None], (size, *x.shape)), axis, 0, 0, tiled=True)


def joined_along(blocks, dim):
    blocks = jnp.moveaxis(blocks, 0, dim)
    dims = blocks.shape
    return blocks.reshape(*dims[:dim], dims[dim] * dims[dim + 1], *dims[dim + 2 :])


def gather_directly(x, axis, dim):
    blocks = from_everyone(x, axis)
    return joined_along(blocks, dim)


def in_one_piece(arrays, axis, split_dim, concat_dim, along):
    widths = [math.prod(a.shape[along:]) for a in arrays]
    both = jnp.concatenate(
        [a.reshape(*a.shape[:along], w) for a, w in zip(arrays, widths)], axis=along
    )
    out = lax.all_to_all(both, axis, split_axis=split_dim, concat_axis=concat_dim, tiled=True)
    blocks = jnp.split(out, [sum(widths[:k]) for k in range(1, len(widths))], axis=along)
    return tuple((b.reshape(*out.shape[:along], *a.shape[along:]) for a, b in zip(arrays, blocks)))


def gathered_once(x, axis):
    leaves = jax.tree.leaves(x)
    turns = sorted(range(len(leaves)), key=lambda k: -leaves[k].size)
    width = (1, *leaves[turns[0]].shape)[-1]
    lines = [
        jnp.pad(leaves[k].reshape(-1), (0, -leaves[k].size % width)).reshape(-1, width)
        for k in turns
    ]
    both, at, found = (from_everyone(jnp.concatenate(lines), axis), 0, {})
    for k, line in zip(turns, lines):
        piece = both[:, at : at + len(line)].reshape(len(both), -1)
        found[k] = piece[:, : leaves[k].size].reshape(-1, *leaves[k].shape)
        at += len(line)
    numbers = iter(range(len(leaves)))
    return jax.tree.map(lambda _: found[next(numbers)], x)


def joined_by_halves(pieces, combine):
    while len(jax.tree.leaves(pieces)[0]) > 1:
        pieces = jax.vmap(combine)(
            *(jax.tree.map(lambda part: part[side::2], pieces) for side in (0, 1))
        )
    return jax.tree.map(lambda part: part[0], pieces)


def joined_all(x, axis, combine):
    pieces = gathered_once(x, axis)
    return joined_by_halves(pieces, combine)


def combine_parts(first_part, second_part):
    first_top, first_total, first_sum = first_part
    second_top, second_total, second_sum = second_part
    merged_top = jnp.maximum(first_top, second_top)
    first_factor = jnp.exp(first_top - merged_top)
    second_factor = jnp.exp(second_top - merged_top)
    merged_total = first_total * first_factor + second_total * second_factor
    merged_sum = first_sum * first_factor[..., None] + second_sum * second_factor[..., None]
    return (merged_top, merged_total, merged_sum)


def normalize(state, norm_gain):
    mean = jnp.mean(state, axis=-1, keepdims=True)
    centered = state - mean
    var = jnp.mean(centered * centered, axis=-1, keepdims=True)
    return centered * lax.rsqrt(var + 1e-05) * norm_gain


def local(
    features,
    conv_weight,
    queries,
    w_query,
    w_key,
    w_value,
    w_out,
    norm_gain,
    mask_weight,
    mask_blocks,
):
    depth_cells, row_cells, x_cells, channels = features.shape
    extended = with_halo(features, (("span", 0), ("qry", 1)), 1)
    padded = jnp.pad(extended, ((0, 0), (0, 0), (1, 1), (0, 0)))
    taps = conv_weight.reshape(3, 3, 3, channels, channels)
    conv = jnp.zeros((depth_cells, row_cells, x_cells, channels), jnp.float32)
    for depth_off in range(3):
        for row_off in range(3):
            slab = padded[
                depth_off : depth_off + depth_cells, row_off : row_off + row_cells
            ].reshape(-1, channels)
            wide_taps = jnp.concatenate(
                [
                    taps[depth_off, row_off, 0],
                    taps[depth_off, row_off, 1],
                    taps[depth_off, row_off, 2],
                ],
                axis=1,
            )
            product = jnp.dot(slab, wide_taps, preferred_element_type=jnp.float32)
            product = product.reshape(depth_cells, row_cells, x_cells + 2, 3, channels)
            conv = (
                conv
                + product[:, :, 0:x_cells, 0]
                + product[:, :, 1 : x_cells + 1, 1]
                + product[:, :, 2 : x_cells + 2, 2]
            )
    pixel = jnp.maximum(conv, 0.0).astype(jnp.bfloat16)
    voxels = depth_cells * row_cells * x_cells
    local_blocks = depth_cells * row_cells
    flat = pixel.reshape(voxels, channels)
    grid_rows = row_cells * lax.axis_size("qry")
    depth_ids = lax.axis_index("span") * depth_cells + jnp.arange(depth_cells, dtype=jnp.int32)
    row_ids = lax.axis_index("qry") * row_cells + jnp.arange(row_cells, dtype=jnp.int32)
    block_ids = (depth_ids[:, None] * grid_rows + row_ids[None, :]).reshape(-1)
    matches = mask_blocks[:, :, None] == block_ids[None, None, :]
    present = jnp.any(matches, axis=1)
    query_count = mask_blocks.shape[0]
    head_dim = channels // HEADS
    scale = head_dim ** (-0.5)
    query_group = 64
    state = queries
    for layer_index in range(LAYERS):
        state_all = gather_directly(state, "qry", 0)
        qproj = (
            (
                jnp.dot(
                    state_all.astype(jnp.bfloat16),
                    w_query[layer_index],
                    preferred_element_type=jnp.float32,
                )
                * scale
            )
            .astype(jnp.bfloat16)
            .reshape(query_count // query_group, query_group, HEADS, head_dim)
        )
        keys = jnp.dot(flat, w_key[layer_index], preferred_element_type=jnp.float32).astype(
            jnp.bfloat16
        )
        values = jnp.dot(flat, w_value[layer_index], preferred_element_type=jnp.float32).astype(
            jnp.bfloat16
        )
        partial_keys = keys
        partial_values = values
        partial_keys = partial_keys.reshape(voxels, HEADS, head_dim)
        partial_values = partial_values.reshape(voxels, HEADS, head_dim)
        present_groups = present.reshape(query_count // query_group, query_group, local_blocks)

        def one_group(operands):
            group_q, group_present = operands
            allowed = jnp.broadcast_to(
                group_present[:, None, :, None], (query_group, 1, local_blocks, x_cells)
            ).reshape(query_group, 1, voxels)
            scores = jnp.einsum(
                "nhe,vhe->nhv", group_q, partial_keys, preferred_element_type=jnp.float32
            )
            local_top = jnp.max(jnp.where(allowed, scores, -1e30), axis=-1)
            prob = jnp.where(allowed, jnp.exp(scores - local_top[..., None]), 0.0)
            local_total = jnp.sum(prob, axis=-1)
            local_sum = jnp.einsum(
                "nhv,vhe->nhe",
                prob.astype(jnp.bfloat16),
                partial_values,
                preferred_element_type=jnp.float32,
            )
            return (local_top, local_total, local_sum)

        group_top, group_total, group_sum = lax.map(one_group, (qproj, present_groups))
        local_top = group_top.reshape(query_count, HEADS)
        local_total = group_total.reshape(query_count, HEADS)
        local_sum = group_sum.reshape(query_count, HEADS, head_dim)
        peer_top, peer_total, peer_sum = in_one_piece(
            (local_top[None], local_total[None], local_sum[None]), "qry", 1, 0, 3
        )
        owner_top = jnp.max(peer_top, axis=0)
        peer_factor = jnp.exp(peer_top - owner_top[None])
        owner_total = jnp.sum(peer_total * peer_factor, axis=0)
        owner_sum = jnp.sum(peer_sum * peer_factor[..., None], axis=0)
        merged_top, merged_total, merged_sum = joined_all(
            (owner_top, owner_total, owner_sum), "span", combine_parts
        )
        rows_here = state.shape[0]
        attn = (
            (merged_sum / merged_total[..., None]).reshape(rows_here, channels).astype(jnp.bfloat16)
        )
        state = state + jnp.dot(attn, w_out[layer_index], preferred_element_type=jnp.float32)
    query_embed = normalize(state, norm_gain)
    embed_all = gather_directly(query_embed, "qry", 0)
    mask_embed = jnp.dot(
        embed_all.astype(jnp.bfloat16), mask_weight, preferred_element_type=jnp.float32
    ).astype(jnp.bfloat16)
    logits = jnp.einsum(
        "nd,vd->nv", mask_embed, flat, preferred_element_type=jnp.float32
    ) * channels ** (-0.5)
    mask_logits = logits.astype(jnp.bfloat16).reshape(query_count, depth_cells, row_cells, x_cells)
    return (query_embed, mask_logits)


def solution(mesh):
    return jax.shard_map(
        local,
        mesh=mesh,
        in_specs=(
            P("span", "qry", None, None),
            P(),
            P("qry", None),
            P(),
            P(),
            P(),
            P(),
            P(),
            P(),
            P(),
        ),
        out_specs=(P("qry", None), P(None, "span", "qry", None)),
        check_vma=False,
    )
```

profile of v0, /device:TPU:1, one launch (start us, length us, event | category | flops | bytes accessed | tf_op | source)
XLA Modules:
  0.0 224.2 jit_solution(11964165383209903682)
XLA Ops:
  0.6 5.1 %collective-permute-start = (bf16[1,2,128,256]{3,2,1,0:T(8,128)(2,1)}, bf16[1,2,128,256]{3,2,1,0:T(8,128)(2,1)}, u32[]{:S(2)}, u32[]{:S(2)}) collective-permute-start(bf16[1,2,128,256]{3,2,1,0:T(8,128)(2,1)} %param.14), channel_id=1, source_target_pairs={{0,16},{16,32},{32,48},{48,64},{64,80},{80,96},{96,112},{112,128},... | collective-permute-start | bytes 393224 | tf_op jit(solution)/shard_map/ppermute | solution.py:20
  5.7 2.2 collective-permute-start.1
  7.9 1.3 broadcast_in_dim.129
  9.2 6.6 %all-to-all-start = ((bf16[16,8,256]{2,1,0:T(8,128)(2,1)}), bf16[16,8,256]{2,1,0:T(8,128)(2,1)}, u32[]{:S(2)}, u32[]{:S(2)}) async-start(bf16[16,8,256]{2,1,0:T(8,128)(2,1)} %broadcast_in_dim.129), calls=%async_computation | async-start | bytes 131072 | tf_op jit(solution)/shard_map/all_to_all | solution.py:31
  15.8 2.5 %fusion.83 = (bf16[1,1,1,256,256]{4,3,2,1,0:T(8,128)(2,1)S(1)}, bf16[1,1,1,256,256]{4,3,2,1,0:T(8,128)(2,1)S(1)}, bf16[1,1,1,256,256]{4,3,2,1,0:T(8,128)(2,1)S(1...) fusion(bf16[3,3,3,256,256]{4,3,2,1,0:T(8,128)(2,1)} %bitcast.420), kind=kLoop, calls=%fused_computation.212 | loop fusion | bytes 4980736 | tf_op jit(solution)/shard_map/slice | solution.py:127
  18.3 1.4 fusion.84
  19.7 1.7 copy.598
  34.4 1.3 pad_maximum_fusion.4
  39.2 0.9 constant_dynamic-update-slice_fusion.2
  40.2 0.9 constant_dynamic-update-slice_fusion
  41.9 3.9 %collective-permute-start.2 = (bf16[3,1,128,256]{3,2,1,0:T(8,128)(2,1)}, bf16[3,1,128,256]{3,2,1,0:T(8,128)(2,1)}, u32[]{:S(2)}, u32[]{:S(2)}) collective-permute-start(bf16[3,1,128,256]{3,2,1,0:T(8,128)(2,1)} %get-tuple-element.350), channel_id=1, source_target_pairs={{0,1},{1,2},{2,3},{3,4},{4,5},{5,6},{6,7},{7,8},{8,9},{9,10},{10,1... | collective-permute-start | bytes 589832 | tf_op jit(solution)/shard_map/ppermute | solution.py:20
  45.8 1.3 collective-permute-start.3
  47.1 1.0 fusion.23
  49.5 4.8 %collective-permute-done.3 = bf16[3,1,128,256]{3,2,1,0:T(8,128)(2,1)} collective-permute-done((bf16[3,1,128,256]{3,2,1,0:T(8,128)(2,1)}, bf16[3,1,128,256]{3,2,1,0:T(8,128)(2,1)}, u32[]{:S(2)}, u32[]{:S(2)}) %collective-permute-start.3) | collective-permute-done | bytes 196640 | tf_op jit(solution)/shard_map/ppermute | solution.py:22
  54.2 1.2 fusion.30
  58.8 1.3 maximum_convert_fusion
  60.7 0.9 convolution_convert_fusion.2
  62.4 14.7 %while.28 = (s32[]{:T(128)}, f32[2,64,8]{1,0,2:T(2,128)S(1)}, f32[2,64,8]{1,0,2:T(2,128)S(1)}, f32[2,64,8,32]{1,0,3,2:T(2,128)}, pred[2,64,2]{1,2,0:T(4,128)(4,1...) while((s32[]{:T(128)}, f32[2,64,8]{1,0,2:T(2,128)S(1)}, ...), condition=%wide.region_4.5_spmd, body=%wide.region_1.4_spmd.sunk | while | flops 17824768 | bytes 2213109 | solution.py:201
  62.7 1.2 select_reduce_fusion.4
  63.9 1.2 fusion.127
  65.1 4.3 %dynamic_update_slice.28 = f32[2,64,8,32]{1,0,3,2:T(2,128)} dynamic-update-slice(f32[2,64,8,32]{1,0,3,2:T(2,128)} %get-tuple-element.480, f32[1,64,8,32]{1,0,3,2:T(1,128)S(1)} %bitcast.402, s32[]{:T(128)} %get-tuple-element.477, s32[]{:T(128)} %constant.58.clone.1..sunk, s32[]{:T(128)} %constant.58.clone.1..sunk, s32[]{:T(128)} %constant.58.clone.1..sunk) | dynamic-update-slice | bytes 131076 | tf_op jit(solution)/shard_map/while/body/jit(dynamic_update_index_in_dim)/dynamic_update_slice | solution.py:201
  70.1 1.2 select_reduce_fusion.4
  71.3 1.2 fusion.127
  72.4 4.3 %dynamic_update_slice.28 = f32[2,64,8,32]{1,0,3,2:T(2,128)} dynamic-update-slice(f32[2,64,8,32]{1,0,3,2:T(2,128)} %get-tuple-element.480, f32[1,64,8,32]{1,0,3,2:T(1,128)S(1)} %bitcast.402, s32[]{:T(128)} %get-tuple-element.477, s32[]{:T(128)} %constant.58.clone.1..sunk, s32[]{:T(128)} %constant.58.clone.1..sunk, s32[]{:T(128)} %constant.58.clone.1..sunk) | dynamic-update-slice | bytes 131076 | tf_op jit(solution)/shard_map/while/body/jit(dynamic_update_index_in_dim)/dynamic_update_slice | solution.py:201
  77.1 1.1 broadcast_in_dim_reshape.7
  79.2 14.0 %all_to_all.49 = f32[16,1,2176]{2,1,0:T(1,128)S(1)} all-to-all(f32[16,1,2176]{2,1,0:T(1,128)S(1)} %reshape.436), channel_id=1, replica_groups=mesh['span'=16,'qry'=16] {'qry'}, dimensions={0} | all-to-all | bytes 278528 | tf_op jit(solution)/shard_map/all_to_all | solution.py:50
  93.7 1.6 reduce.14
  95.4 1.4 reshape.437
  96.8 1.2 slice_reduce_fusion.1
  98.0 1.5 copy.610
  100.2 1.5 copy.524
  103.0 11.6 %all-to-all-start.2 = ((f32[16,68,32]{1,2,0:T(8,128)}), f32[16,68,32]{1,2,0:T(8,128)S(1)}, u32[]{:S(2)}, u32[]{:S(2)}) async-start(f32[16,68,32]{1,2,0:T(8,128)} %broadcast_in_dim.130), calls=%async_computation.2 | async-start | bytes 524288 | tf_op jit(solution)/shard_map/all_to_all | solution.py:31
  114.8 11.5 %all-to-all-done.2 = f32[16,68,32]{1,2,0:T(8,128)S(1)} async-done(((f32[16,68,32]{1,2,0:T(8,128)}), f32[16,68,32]{1,2,0:T(8,128)S(1)}, u32[]{:S(2)}, u32[]{:S(2)}) %all-to-all-start.2) | async-done | bytes 139296 | tf_op jit(solution)/shard_map/all_to_all | solution.py:31
  126.3 0.9 fusion.90
  127.1 1.2 copy.612
  132.8 1.5 copy.532
  134.2 1.5 copy.533
  137.4 1.0 copy.611
  138.6 1.2 multiply_add_fusion.1
  143.2 3.5 %all-to-all-start.3 = ((bf16[16,8,256]{2,1,0:T(8,128)(2,1)}), bf16[16,8,256]{2,1,0:T(8,128)(2,1)S(1)}, u32[]{:S(2)}, u32[]{:S(2)}) async-start(bf16[16,8,256]{2,1,0:T(8,128)(2,1)} %broadcast_in_dim.131), calls=%async_computation.3 | async-start | bytes 131072 | tf_op jit(solution)/shard_map/all_to_all | solution.py:31
  146.7 0.9 convolution_convert_fusion
  147.6 6.2 %all-to-all-done.3 = bf16[16,8,256]{2,1,0:T(8,128)(2,1)S(1)} async-done(((bf16[16,8,256]{2,1,0:T(8,128)(2,1)}), bf16[16,8,256]{2,1,0:T(8,128)(2,1)S(1)}, u32[]{:S(2)}, u32[]{:S(2)}) %all-to-all-start.3) | async-done | bytes 65568 | tf_op jit(solution)/shard_map/all_to_all | solution.py:31
  153.8 1.1 fusion.24
  156.6 14.7 %while.29 = (s32[]{:T(128)}, f32[2,64,8]{1,0,2:T(2,128)S(1)}, f32[2,64,8]{1,0,2:T(2,128)S(1)}, f32[2,64,8,32]{1,0,3,2:T(2,128)}, pred[2,64,2]{1,2,0:T(4,128)(4,1...) while((s32[]{:T(128)}, f32[2,64,8]{1,0,2:T(2,128)S(1)}, ...), condition=%wide.region_11.12_spmd, body=%wide.region_8.11_spmd.sunk | while | flops 17824768 | bytes 2213109 | solution.py:201
  156.9 1.2 select_reduce_fusion.5
  158.1 1.2 fusion.132
  159.3 4.3 %dynamic_update_slice.31 = f32[2,64,8,32]{1,0,3,2:T(2,128)} dynamic-update-slice(f32[2,64,8,32]{1,0,3,2:T(2,128)} %get-tuple-element.510, f32[1,64,8,32]{1,0,3,2:T(1,128)S(1)} %bitcast.403, s32[]{:T(128)} %get-tuple-element.507, s32[]{:T(128)} %constant.58.clone.1..sunk.1, s32[]{:T(128)} %constant.58.clone.1..sunk.1, s32[]{:T(128)} %constant.58.clone.1..sunk.1) | dynamic-update-slice | bytes 131076 | tf_op jit(solution)/shard_map/while/body/jit(dynamic_update_index_in_dim)/dynamic_update_slice | solution.py:201
  164.2 1.2 select_reduce_fusion.5
  165.4 1.2 fusion.132
  166.6 4.3 %dynamic_update_slice.31 = f32[2,64,8,32]{1,0,3,2:T(2,128)} dynamic-update-slice(f32[2,64,8,32]{1,0,3,2:T(2,128)} %get-tuple-element.510, f32[1,64,8,32]{1,0,3,2:T(1,128)S(1)} %bitcast.403, s32[]{:T(128)} %get-tuple-element.507, s32[]{:T(128)} %constant.58.clone.1..sunk.1, s32[]{:T(128)} %constant.58.clone.1..sunk.1, s32[]{:T(128)} %constant.58.clone.1..sunk.1) | dynamic-update-slice | bytes 131076 | tf_op jit(solution)/shard_map/while/body/jit(dynamic_update_index_in_dim)/dynamic_update_slice | solution.py:201
  171.3 1.1 broadcast_in_dim_reshape.8
  173.4 9.7 %all_to_all.50 = f32[16,1,2176]{2,1,0:T(1,128)S(1)} all-to-all(f32[16,1,2176]{2,1,0:T(1,128)S(1)} %reshape.438), channel_id=1, replica_groups=mesh['span'=16,'qry'=16] {'qry'}, dimensions={0} | all-to-all | bytes 278528 | tf_op jit(solution)/shard_map/all_to_all | solution.py:50
  183.0 1.0 reduce.15
  184.5 1.2 slice_reduce_fusion
  185.7 1.5 copy.614
  187.9 1.5 copy.548
  190.7 5.2 %all-to-all-start.5 = ((f32[16,68,32]{1,2,0:T(8,128)}), f32[16,68,32]{1,2,0:T(8,128)S(1)}, u32[]{:S(2)}, u32[]{:S(2)}) async-start(f32[16,68,32]{1,2,0:T(8,128)} %broadcast_in_dim.132), calls=%async_computation.5 | async-start | bytes 524288 | tf_op jit(solution)/shard_map/all_to_all | solution.py:31
  195.9 1.0 fusion.85
  196.9 1.7 slice.563
  198.6 0.9 fusion.87
  199.5 8.2 %all-to-all-done.5 = f32[16,68,32]{1,2,0:T(8,128)S(1)} async-done(((f32[16,68,32]{1,2,0:T(8,128)}), f32[16,68,32]{1,2,0:T(8,128)S(1)}, u32[]{:S(2)}, u32[]{:S(2)}) %all-to-all-start.5) | async-done | bytes 139296 | tf_op jit(solution)/shard_map/all_to_all | solution.py:31
  213.0 3.5 %all-to-all-start.6 = ((bf16[16,8,256]{2,1,0:T(8,128)(2,1)}), bf16[16,8,256]{2,1,0:T(8,128)(2,1)S(1)}, u32[]{:S(2)}, u32[]{:S(2)}) async-start(bf16[16,8,256]{2,1,0:T(8,128)(2,1)} %broadcast_in_dim.133), calls=%async_computation.6 | async-start | bytes 131072 | tf_op jit(solution)/shard_map/all_to_all | solution.py:31
  216.6 1.2 fusion.34
  217.8 5.5 %all-to-all-done.6 = bf16[16,8,256]{2,1,0:T(8,128)(2,1)S(1)} async-done(((bf16[16,8,256]{2,1,0:T(8,128)(2,1)}), bf16[16,8,256]{2,1,0:T(8,128)(2,1)S(1)}, u32[]{:S(2)}, u32[]{:S(2)}) %all-to-all-start.6) | async-done | bytes 65568 | tf_op jit(solution)/shard_map/all_to_all | solution.py:31
  (277 shorter events, 49.8 us)
Async XLA Ops:
  0.6 222.6 %copy-start = (bf16[256,256]{1,0:T(8,128)(2,1)S(1)}, bf16[256,256]{1,0:T(8,128)(2,1)}, u32[]{:S(2)}) copy-start(bf16[256,256]{1,0:T(8,128)(2,1)} %param.22) | copy-start | bytes 393220
  0.6 38.6 %collective-permute-start = (bf16[1,2,128,256]{3,2,1,0:T(8,128)(2,1)}, bf16[1,2,128,256]{3,2,1,0:T(8,128)(2,1)}, u32[]{:S(2)}, u32[]{:S(2)}) collective-permute-start(bf16[1,2,128,256]{3,2,1,0:T(8,128)(2,1)} %param.14), channel_id=1, source_target_pairs={{0,16},{16,32},{32,48},{48,64},{64,80},{80,96},{96,112},{112,128},... | collective-permute-start | bytes 393224 | tf_op jit(solution)/shard_map/ppermute | solution.py:20
  5.7 34.5 %collective-permute-start.1 = (bf16[1,2,128,256]{3,2,1,0:T(8,128)(2,1)}, bf16[1,2,128,256]{3,2,1,0:T(8,128)(2,1)}, u32[]{:S(2)}, u32[]{:S(2)}) collective-permute-start(bf16[1,2,128,256]{3,2,1,0:T(8,128)(2,1)} %param.14), channel_id=1, source_target_pairs={{16,0},{32,16},{48,32},{64,48},{80,64},{96,80},{112,96},{128,112},... | collective-permute-start | bytes 393224 | tf_op jit(solution)/shard_map/ppermute | solution.py:22
  9.2 37.9 %all-to-all-start = ((bf16[16,8,256]{2,1,0:T(8,128)(2,1)}), bf16[16,8,256]{2,1,0:T(8,128)(2,1)}, u32[]{:S(2)}, u32[]{:S(2)}) async-start(bf16[16,8,256]{2,1,0:T(8,128)(2,1)} %broadcast_in_dim.129), calls=%async_computation | async-start | bytes 131072 | tf_op jit(solution)/shard_map/all_to_all | solution.py:31
  24.4 9.8 %copy-start.14 = (bf16[1,1,1,256,256]{3,4,2,1,0:T(8,128)(2,1)S(1)}, bf16[1,1,1,256,256]{3,4,2,1,0:T(8,128)(2,1)}, u32[]{:S(2)}) copy-start(bf16[1,1,1,256,256]{3,4,2,1,0:T(8,128)(2,1)} %copy.598) | copy-start | bytes 393220
  24.4 9.8 %copy-start.15 = (bf16[1,1,1,256,256]{3,4,2,1,0:T(8,128)(2,1)S(1)}, bf16[1,1,1,256,256]{3,4,2,1,0:T(8,128)(2,1)}, u32[]{:S(2)}) copy-start(bf16[1,1,1,256,256]{3,4,2,1,0:T(8,128)(2,1)} %copy.599) | copy-start | bytes 393220
  31.1 3.2 %copy-start.16 = (bf16[1,1,1,256,256]{3,4,2,1,0:T(8,128)(2,1)S(1)}, bf16[1,1,1,256,256]{3,4,2,1,0:T(8,128)(2,1)}, u32[]{:S(2)}) copy-start(bf16[1,1,1,256,256]{3,4,2,1,0:T(8,128)(2,1)} %copy.592) | copy-start | bytes 393220
  31.1 3.2 %copy-start.17 = (bf16[1,1,1,256,256]{3,4,2,1,0:T(8,128)(2,1)S(1)}, bf16[1,1,1,256,256]{3,4,2,1,0:T(8,128)(2,1)}, u32[]{:S(2)}) copy-start(bf16[1,1,1,256,256]{3,4,2,1,0:T(8,128)(2,1)} %copy.593) | copy-start | bytes 393220
  31.1 3.2 %copy-start.18 = (bf16[1,1,1,256,256]{3,4,2,1,0:T(8,128)(2,1)S(1)}, bf16[1,1,1,256,256]{3,4,2,1,0:T(8,128)(2,1)}, u32[]{:S(2)}) copy-start(bf16[1,1,1,256,256]{3,4,2,1,0:T(8,128)(2,1)} %copy.594) | copy-start | bytes 393220
  34.2 1.5 copy-start.19
  34.2 1.5 copy-start.20
  34.2 1.5 copy-start.21
  34.2 1.5 copy-start.22
  34.3 1.5 copy-start.23
  34.3 1.5 copy-start.24
  34.3 2.3 %copy-start.25 = (bf16[1,1,1,256,256]{3,4,2,1,0:T(8,128)(2,1)S(1)}, bf16[1,1,1,256,256]{3,4,2,1,0:T(8,128)(2,1)}, u32[]{:S(2)}) copy-start(bf16[1,1,1,256,256]{3,4,2,1,0:T(8,128)(2,1)} %copy.591) | copy-start | bytes 393220
  34.3 2.3 %copy-start.26 = (bf16[1,1,1,256,256]{3,4,2,1,0:T(8,128)(2,1)S(1)}, bf16[1,1,1,256,256]{3,4,2,1,0:T(8,128)(2,1)}, u32[]{:S(2)}) copy-start(bf16[1,1,1,256,256]{3,4,2,1,0:T(8,128)(2,1)} %copy.589) | copy-start | bytes 393220
  34.3 2.3 %copy-start.27 = (bf16[1,1,1,256,256]{3,4,2,1,0:T(8,128)(2,1)S(1)}, bf16[1,1,1,256,256]{3,4,2,1,0:T(8,128)(2,1)}, u32[]{:S(2)}) copy-start(bf16[1,1,1,256,256]{3,4,2,1,0:T(8,128)(2,1)} %copy.590) | copy-start | bytes 393220
  34.4 3.0 %copy-start.37 = (s32[128,4]{0,1:T(4,128)S(1)}, s32[128,4]{0,1:T(4,128)}, u32[]{:S(2)}) copy-start(s32[128,4]{0,1:T(4,128)} %param.23) | copy-start | bytes 6148
  35.8 4.4 %copy-start.35 = (bf16[1,2,128,256]{3,2,1,0:T(8,128)(2,1)S(1)}, bf16[1,2,128,256]{3,2,1,0:T(8,128)(2,1)}, u32[]{:S(2)}) copy-start(bf16[1,2,128,256]{3,2,1,0:T(8,128)(2,1)} %param.14) | copy-start | bytes 393220
  37.4 9.7 %copy-start.34 = (bf16[2,256,256]{2,1,0:T(8,128)(2,1)S(1)}, bf16[2,256,256]{2,1,0:T(8,128)(2,1)}, u32[]{:S(2)}) copy-start(bf16[2,256,256]{2,1,0:T(8,128)(2,1)} %param.17) | copy-start | bytes 786436
  41.9 7.6 %collective-permute-start.2 = (bf16[3,1,128,256]{3,2,1,0:T(8,128)(2,1)}, bf16[3,1,128,256]{3,2,1,0:T(8,128)(2,1)}, u32[]{:S(2)}, u32[]{:S(2)}) collective-permute-start(bf16[3,1,128,256]{3,2,1,0:T(8,128)(2,1)} %get-tuple-element.350), channel_id=1, source_target_pairs={{0,1},{1,2},{2,3},{3,4},{4,5},{5,6},{6,7},{7,8},{8,9},{9,10},{10,1... | collective-permute-start | bytes 589832 | tf_op jit(solution)/shard_map/ppermute | solution.py:20
  45.8 8.5 %collective-permute-start.3 = (bf16[3,1,128,256]{3,2,1,0:T(8,128)(2,1)}, bf16[3,1,128,256]{3,2,1,0:T(8,128)(2,1)}, u32[]{:S(2)}, u32[]{:S(2)}) collective-permute-start(bf16[3,1,128,256]{3,2,1,0:T(8,128)(2,1)} %get-tuple-element.351), channel_id=1, source_target_pairs={{1,0},{2,1},{3,2},{4,3},{5,4},{6,5},{7,6},{8,7},{9,8},{10,9},{11,1... | collective-permute-start | bytes 589832 | tf_op jit(solution)/shard_map/ppermute | solution.py:22
  55.8 2.9 %copy-start.1 = (f32[1,2,130,3,256]{4,2,3,1,0:T(8,128)}, f32[1,2,130,3,256]{4,2,3,1,0:T(8,128)S(1)}, u32[]{:S(2)}) copy-start(f32[1,2,130,3,256]{4,2,3,1,0:T(8,128)S(1)} %convolution_bitcast_fusion.5) | copy-start | bytes 2396164
  56.7 1.0 copy-start.4
  57.0 1.0 copy-start.5
  57.4 1.1 copy-start.6
  58.7 1.3 copy-start.28
  58.7 2.0 copy-start.30
  58.8 3.7 %copy-start.39 = (pred[2,64,2]{1,2,0:T(4,128)(4,1)S(1)}, pred[2,64,2]{1,2,0:T(4,128)(4,1)}, u32[]{:S(2)}) copy-start(pred[2,64,2]{1,2,0:T(4,128)(4,1)} %copy.514) | copy-start | bytes 772
  60.1 0.7 copy-start.2
  98.0 16.6 %copy-start.3 = (bf16[1,2,128,1,256]{4,2,3,1,0:T(8,128)(2,1)S(1)}, bf16[1,2,128,1,256]{4,2,3,1,0:T(8,128)(2,1)}, u32[]{:S(2)}) copy-start(bf16[1,2,128,1,256]{4,2,3,1,0:T(8,128)(2,1)} %copy-done.2) | copy-start | bytes 393220
  100.1 14.4 %copy-start.29 = (bf16[2,256,256]{2,1,0:T(8,128)(2,1)S(1)}, bf16[2,256,256]{2,1,0:T(8,128)(2,1)}, u32[]{:S(2)}) copy-start(bf16[2,256,256]{2,1,0:T(8,128)(2,1)} %param.18) | copy-start | bytes 786436
  103.0 23.3 %all-to-all-start.2 = ((f32[16,68,32]{1,2,0:T(8,128)}), f32[16,68,32]{1,2,0:T(8,128)S(1)}, u32[]{:S(2)}, u32[]{:S(2)}) async-start(f32[16,68,32]{1,2,0:T(8,128)} %broadcast_in_dim.130), calls=%async_computation.2 | async-start | bytes 524288 | tf_op jit(solution)/shard_map/all_to_all | solution.py:31
  131.3 15.4 %copy-start.31 = (bf16[2,256,256]{2,1,0:T(8,128)(2,1)S(1)}, bf16[2,256,256]{2,1,0:T(8,128)(2,1)}, u32[]{:S(2)}) copy-start(bf16[2,256,256]{2,1,0:T(8,128)(2,1)} %param.19) | copy-start | bytes 786436
  138.4 3.3 %copy-start.32 = (bf16[2,256,256]{2,1,0:T(8,128)(2,1)S(1)}, bf16[2,256,256]{2,1,0:T(8,128)(2,1)}, u32[]{:S(2)}) copy-start(bf16[2,256,256]{2,1,0:T(8,128)(2,1)} %param.20) | copy-start | bytes 786436
  139.8 16.8 %copy-start.40 = (pred[2,64,2]{1,2,0:T(4,128)(4,1)S(1)}, pred[2,64,2]{1,2,0:T(4,128)(4,1)}, u32[]{:S(2)}) copy-start(pred[2,64,2]{1,2,0:T(4,128)(4,1)} %copy.514) | copy-start | bytes 772
  143.2 10.6 %all-to-all-start.3 = ((bf16[16,8,256]{2,1,0:T(8,128)(2,1)}), bf16[16,8,256]{2,1,0:T(8,128)(2,1)S(1)}, u32[]{:S(2)}, u32[]{:S(2)}) async-start(bf16[16,8,256]{2,1,0:T(8,128)(2,1)} %broadcast_in_dim.131), calls=%async_computation.3 | async-start | bytes 131072 | tf_op jit(solution)/shard_map/all_to_all | solution.py:31
  190.7 17.1 %all-to-all-start.5 = ((f32[16,68,32]{1,2,0:T(8,128)}), f32[16,68,32]{1,2,0:T(8,128)S(1)}, u32[]{:S(2)}, u32[]{:S(2)}) async-start(f32[16,68,32]{1,2,0:T(8,128)} %broadcast_in_dim.132), calls=%async_computation.5 | async-start | bytes 524288 | tf_op jit(solution)/shard_map/all_to_all | solution.py:31
  209.8 2.5 %copy-start.38 = (f32[256]{0:T(256)S(1)}, f32[256]{0:T(256)}, u32[]{:S(2)}) copy-start(f32[256]{0:T(256)} %param.21) | copy-start | bytes 3076
  209.9 6.6 %copy-start.7 = (f32[1,2,128,1,256]{4,2,3,1,0:T(8,128)S(1)}, f32[1,2,128,1,256]{4,2,3,1,0:T(8,128)}, u32[]{:S(2)}) copy-start(f32[1,2,128,1,256]{4,2,3,1,0:T(8,128)} %get-tuple-element.303) | copy-start | bytes 786436
  209.9 6.6 %copy-start.8 = (f32[1,2,128,1,256]{4,2,3,1,0:T(8,128)S(1)}, f32[1,2,128,1,256]{4,2,3,1,0:T(8,128)}, u32[]{:S(2)}) copy-start(f32[1,2,128,1,256]{4,2,3,1,0:T(8,128)} %get-tuple-element.337) | copy-start | bytes 786436
  209.9 6.6 %copy-start.9 = (f32[1,2,128,1,256]{4,2,3,1,0:T(8,128)S(1)}, f32[1,2,128,1,256]{4,2,3,1,0:T(8,128)}, u32[]{:S(2)}) copy-start(f32[1,2,128,1,256]{4,2,3,1,0:T(8,128)} %get-tuple-element.358) | copy-start | bytes 786436
  210.0 6.6 %copy-start.10 = (f32[1,2,128,1,256]{4,2,3,1,0:T(8,128)S(1)}, f32[1,2,128,1,256]{4,2,3,1,0:T(8,128)}, u32[]{:S(2)}) copy-start(f32[1,2,128,1,256]{4,2,3,1,0:T(8,128)} %get-tuple-element.359) | copy-start | bytes 786436
  210.0 6.6 %copy-start.11 = (f32[1,2,128,1,256]{4,2,3,1,0:T(8,128)S(1)}, f32[1,2,128,1,256]{4,2,3,1,0:T(8,128)}, u32[]{:S(2)}) copy-start(f32[1,2,128,1,256]{4,2,3,1,0:T(8,128)} %get-tuple-element.360) | copy-start | bytes 786436
  210.0 6.6 %copy-start.12 = (f32[1,2,128,1,256]{4,2,3,1,0:T(8,128)S(1)}, f32[1,2,128,1,256]{4,2,3,1,0:T(8,128)}, u32[]{:S(2)}) copy-start(f32[1,2,128,1,256]{4,2,3,1,0:T(8,128)} %slice.563) | copy-start | bytes 786436
  210.0 6.6 %copy-start.13 = (f32[1,2,128,1,256]{4,2,3,1,0:T(8,128)S(1)}, f32[1,2,128,1,256]{4,2,3,1,0:T(8,128)}, u32[]{:S(2)}) copy-start(f32[1,2,128,1,256]{4,2,3,1,0:T(8,128)} %get-tuple-element.341) | copy-start | bytes 786436
  210.9 1.0 copy-start.33
  212.4 11.2 %copy-start.36 = (f32[8,256]{1,0:T(8,128)}, f32[8,256]{1,0:T(8,128)S(1)}, u32[]{:S(2)}) copy-start(f32[8,256]{1,0:T(8,128)S(1)} %multiply_multiply_fusion) | copy-start | bytes 24580
  213.0 10.2 %all-to-all-start.6 = ((bf16[16,8,256]{2,1,0:T(8,128)(2,1)}), bf16[16,8,256]{2,1,0:T(8,128)(2,1)S(1)}, u32[]{:S(2)}, u32[]{:S(2)}) async-start(bf16[16,8,256]{2,1,0:T(8,128)(2,1)} %broadcast_in_dim.133), calls=%async_computation.6 | async-start | bytes 131072 | tf_op jit(solution)/shard_map/all_to_all | solution.py:31
where the time goes:
time: 227 us; the launch traced here: 224 us
  local copies, waits for them, and re-layouts  80.7 us (36%)
  starting transfers between devices  42.8 us (19%)
  waiting for transfers between devices  36.6 us (16%)
  blocking collectives  23.7 us (10%)
  other arithmetic  20.5 us (9%)
  matrix products  17.9 us (8%)
    all_to_all x5, waiting for transfers between devices, from_everyone(): lax.all_to_all(jnp.broadcast_to(x[None], (size, *x.shape)), axis, 0, 0, t...  31.4 us
    all_to_all x5, starting transfers between devices, from_everyone(): lax.all_to_all(jnp.broadcast_to(x[None], (size, *x.shape)), axis, 0, 0, t...  30.4 us
    unnamed x123, local copies, waits for them, and re-layouts  26.1 us
    all_to_all x2, blocking collectives, in_one_piece(): lax.all_to_all(both, axis, split_axis=split_dim, concat_axis=concat_dim,...  23.7 us
    dynamic_update_slice x12, local copies, waits for them, and re-layouts, local(): lax.map(one_group, (qproj, present_groups))  17.5 us
    ppermute x2, starting transfers between devices, with_halo(): lax.ppermute(tail, axis, [(i, (i + 1) % count) for i in range(ends)])  8.96 us
    dot_general x4, matrix products, one_group(): jnp.einsum('nhe,vhe->nhv', group_q, partial_keys, preferred_element_type=...  4.81 us
    ppermute x2, waiting for transfers between devices, with_halo(): lax.ppermute(head, axis, [((i + 1) % count, i) for i in range(ends)])  4.77 us
  transfers between devices with their start and end apart: 9, of which 6 were waited for; matrix products, arithmetic and copies ran while one was open for 16% of the time, Pallas kernels for 0%

commit v1 on v0

v1 whole, which is shorter than its diff:
```python
import jax
import jax.numpy as jnp
from jax import lax
from jax.experimental import pallas as pl
from jax.experimental.pallas import tpu as pltpu
from jax.sharding import PartitionSpec as P

MESH = pl.DeviceIdType.MESH
HEADS = 8
LAYERS = 2
D = 256
HEAD_DIM = 32
NX = 128
NQ = 128
MB = 4
NY = 32
SPAN = 16
QRY = 16
F32 = jnp.float32
BF16 = jnp.bfloat16
MSG = 80


def iota(shape, dim):
    return lax.broadcasted_iota(jnp.int32, shape, dim)


def dot(a, b):
    return jnp.dot(a, b, preferred_element_type=F32)


def dot_nt(a, b):
    return lax.dot_general(a, b, (((1,), (1,)), ((), ())), preferred_element_type=F32)


def wrap(i, n):
    return lax.rem(i + n, n)


def merge(ids, block):
    rows = ids.shape[0]
    outs = jnp.concatenate(
        [block[:, half * 32 : half * 32 + 32, :].reshape(QRY * 32, 128) for half in range(2)], axis=1
    )
    terms = block[:, 64:MSG, :].reshape(QRY * 16, 128)
    col = iota((rows, QRY * 32), 1)
    pair_id = (col % 16) * NY + (col // 32) * 2 + (col // 16) % 2
    row = iota((rows, QRY * 16), 1)
    kind = row % 16
    term_y = jnp.where(kind < 6, (row // 16) * 2 + jnp.where(kind < 3, 0, 1), -1)
    lane_z = iota((rows, 128), 1) // HEADS
    pick, term = [], []
    for j in range(MB):
        idj = ids[:, j : j + 1]
        pick.append(jnp.where(pair_id == idj, 1.0, 0.0).astype(BF16))
        term.append(jnp.where(term_y == idj % NY, 1.0, 0.0).astype(BF16))
    chosen = dot(jnp.concatenate(pick, axis=0), outs)
    lse = dot(jnp.concatenate(term, axis=0), terms)
    lses = []
    for j in range(MB):
        lj = jnp.where(lane_z == ids[:, j : j + 1] // NY, lse[j * rows : (j + 1) * rows], 0.0)
        for shift in (8, 16, 32, 64):
            lj = lj + pltpu.roll(lj, shift, axis=1)
        lses.append(lj)
    top = jnp.maximum(jnp.maximum(lses[0], lses[1]), jnp.maximum(lses[2], lses[3]))
    weights = [jnp.exp(lj - top) for lj in lses]
    inv = 1.0 / (weights[0] + weights[1] + weights[2] + weights[3])
    attn = jnp.zeros((rows, D), F32)
    for j in range(MB):
        wj = weights[j] * inv
        attn = attn + jnp.concatenate([wj, wj], axis=1) * chosen[j * rows : (j + 1) * rows]
    return attn


def kernel(
    feat_hbm, conv_hbm, queries_hbm, wq_hbm, wk_hbm, wv_hbm, wo_hbm, gain_ref, mw_hbm, mb_ref,
    embed_ref, logit_ref,
    ext, taps, qbuf, wq, wk, wv, wo, mw, wvp, wop, pix, keys, vals, stage1, stage2, state,
    local_sem, conv_sem, halo_send, halo_recv, q_send, q_recv, s_send, s_recv, y_send, y_recv,
):
    s = lax.axis_index("span")
    q = lax.axis_index("qry")
    up, down = wrap(s + 1, SPAN), wrap(s - 1, SPAN)
    right, left = wrap(q + 1, QRY), wrap(q - 1, QRY)

    own = pltpu.make_async_copy(feat_hbm.at[0], ext.at[1, pl.ds(1, 2)], local_sem.at[0])
    own.start()
    own_q = pltpu.make_async_copy(queries_hbm, qbuf.at[q], local_sem.at[1])
    own_q.start()
    loads = []
    for k, (src, dst) in enumerate(
        ((wv_hbm, wv), (wo_hbm, wo), (wq_hbm, wq), (wk_hbm, wk), (mw_hbm, mw))
    ):
        loads.append(pltpu.make_async_copy(src, dst, local_sem.at[2 + k]))
        loads[-1].start()
    conv_loads = [
        pltpu.make_async_copy(conv_hbm.at[:, dx], taps.at[dx], conv_sem.at[dx]) for dx in range(3)
    ]
    for load in conv_loads:
        load.start()

    barrier = pltpu.get_barrier_semaphore()
    corners = ((up, right), (up, left), (down, right), (down, left))
    for peer in corners:
        pl.semaphore_signal(barrier, inc=1, device_id=peer, device_id_type=MESH)
    for d in range(1, SPAN):
        pl.semaphore_signal(barrier, inc=1, device_id=(wrap(s + d, SPAN), q), device_id_type=MESH)
    for d in range(1, QRY):
        pl.semaphore_signal(barrier, inc=1, device_id=(s, wrap(q + d, QRY)), device_id_type=MESH)
    pl.semaphore_wait(barrier, len(corners) + SPAN - 1 + QRY - 1)

    own.wait()
    sends = []
    both, first, last = ext.at[1, pl.ds(1, 2)], ext.at[1, 1], ext.at[1, 2]
    for k, (src, dst, peer) in enumerate(
        (
            (last, ext.at[0, 0], (up, right)),
            (first, ext.at[0, 3], (up, left)),
            (last, ext.at[2, 0], (down, right)),
            (first, ext.at[2, 3], (down, left)),
            (both, ext.at[0, pl.ds(1, 2)], (up, q)),
            (both, ext.at[2, pl.ds(1, 2)], (down, q)),
            (last, ext.at[1, 0], (s, right)),
            (first, ext.at[1, 3], (s, left)),
        )
    ):
        copy = pltpu.make_async_remote_copy(
            src_ref=src, dst_ref=dst, send_sem=halo_send.at[k], recv_sem=halo_recv.at[k],
            device_id=peer, device_id_type=MESH,
        )
        copy.start()
        sends.append(copy)

    def to_all(buf, me, send_sem, recv_sem, along_span):
        n = SPAN if along_span else QRY
        for d in range(1, n):
            peer = (wrap(s + d, n), q) if along_span else (s, wrap(q + d, n))
            pltpu.make_async_remote_copy(
                src_ref=buf.at[me], dst_ref=buf.at[me], send_sem=send_sem, recv_sem=recv_sem,
                device_id=peer, device_id_type=MESH,
            ).start()

    def wait_all(buf, sem):
        most = buf.at[pl.ds(0, buf.shape[0] - 1)]
        pltpu.make_async_copy(most, most, sem).wait()

    own_q.wait()
    to_all(qbuf, q, q_send, q_recv, False)

    perm = jnp.where(
        iota((D, D), 1) == (iota((D, D), 0) % HEAD_DIM) * HEADS + iota((D, D), 0) // HEAD_DIM, 1.0, 0.0
    ).astype(BF16)
    perm_t = jnp.where(
        iota((D, D), 0) == (iota((D, D), 1) % HEAD_DIM) * HEADS + iota((D, D), 1) // HEAD_DIM, 1.0, 0.0
    ).astype(BF16)
    for load in loads:
        load.wait()
    for layer in range(LAYERS):
        wvp[layer] = dot(wv[layer], perm).astype(BF16)
        wop[layer] = dot(perm_t, wo[layer]).astype(BF16)
    for load in conv_loads:
        load.wait()

    for copy in sends:
        copy.wait_recv()

    @pl.when(s == 0)
    def _():
        ext[0] = jnp.zeros((4, NX, D), BF16)

    @pl.when(s == SPAN - 1)
    def _():
        ext[2] = jnp.zeros((4, NX, D), BF16)

    @pl.when(q == 0)
    def _():
        ext[:, 0] = jnp.zeros((3, NX, D), BF16)

    @pl.when(q == QRY - 1)
    def _():
        ext[:, 3] = jnp.zeros((3, NX, D), BF16)

    slab = jnp.concatenate(
        [ext[dz, dy : dy + 2].reshape(2 * NX, D) for dz in range(3) for dy in range(3)], axis=1
    )
    x_at = iota((2 * NX, D), 0) % NX
    before = dot(slab, taps[0].reshape(9 * D, D))
    conv = jnp.where(x_at == 0, 0.0, pltpu.roll(before, 1, axis=0))
    conv = conv + dot(slab, taps[1].reshape(9 * D, D))
    after = dot(slab, taps[2].reshape(9 * D, D))
    conv = conv + jnp.where(x_at == NX - 1, 0.0, pltpu.roll(after, 2 * NX - 1, axis=0))
    pixel = jnp.maximum(conv, 0.0).astype(BF16)
    pix[...] = pixel
    for layer in range(LAYERS):
        keys[layer] = dot(pixel, wk[layer]).astype(BF16)
        vals[layer] = dot(pixel, wvp[layer]).astype(BF16)

    wait_all(qbuf, q_recv)
    all_ids = mb_ref[...]
    state_all = qbuf[...].reshape(NQ, D)
    own_ids, own_state = [], []
    for r in range(2):
        block_id = s * NY + q * 2 + r
        lists = jnp.max(jnp.where(all_ids == block_id, 1, 0), axis=1, keepdims=True) > 0
        own_ids.append(jnp.sum(jnp.where(lists, all_ids.astype(F32), 0.0), axis=0, keepdims=True))
        own_state.append(jnp.sum(jnp.where(lists, state_all, 0.0), axis=0, keepdims=True))
    own_ids = jnp.concatenate(own_ids + [jnp.full((6, MB), -1.0, F32)], axis=0).astype(jnp.int32)
    own_state = jnp.concatenate(own_state + [jnp.zeros((6, D), F32)], axis=0)

    head_of = iota((HEADS, D), 1) // HEAD_DIM == iota((HEADS, D), 0)
    head_of_lane = iota((HEADS, D), 1) % HEADS == iota((HEADS, D), 0)
    lse_lane = iota((HEADS, 128), 1) == s * HEADS + iota((HEADS, 128), 0)
    for layer in range(LAYERS):
        qproj = (dot(own_state.astype(BF16), wq[layer]) * HEAD_DIM**-0.5).astype(BF16).astype(F32)
        spread = jnp.concatenate(
            [jnp.where(head_of, qproj[r : r + 1], 0.0) for r in range(2)], axis=0
        ).astype(BF16)
        scores = dot_nt(spread, keys[layer])
        scores = jnp.concatenate([scores[0:8, 0:NX], scores[8:16, NX : 2 * NX]], axis=0)
        top = jnp.max(scores, axis=1, keepdims=True)
        prob = jnp.exp(scores - top)
        total = jnp.sum(prob, axis=1, keepdims=True)
        inv = 1.0 / total
        lse = top + jnp.log(total)
        prob = prob.astype(BF16)
        low, high, lines = [], [], []
        for r in range(2):
            part = slice(r * HEADS, (r + 1) * HEADS)
            weighted = dot(prob[part], vals[layer, r * NX : (r + 1) * NX])
            out = jnp.sum(jnp.where(head_of_lane, weighted * inv[part], 0.0), axis=0, keepdims=True)
            low.append(out[:, 0:128])
            high.append(out[:, 128:256])
            lines.append(jnp.sum(jnp.where(lse_lane, lse[part], 0.0), axis=0, keepdims=True))
        buf1, buf2 = stage1.at[layer], stage2.at[layer]
        buf1[s] = jnp.concatenate(low + high + lines + [jnp.zeros((2, 128), F32)], axis=0)
        to_all(buf1, s, s_send.at[layer], s_recv.at[layer], True)
        if layer == 1:
            attn = merge(all_ids, stage2[0])
            state[...] = state_all + dot(attn.astype(BF16), wop[0])
        wait_all(buf1, s_recv.at[layer])
        got = stage1[layer]
        message = [got[:, k, :] for k in range(4)]
        for r in range(2):
            line = jnp.sum(got[:, 4 + r, :], axis=0, keepdims=True)
            for _ in range(3):
                term = line.astype(BF16).astype(F32)
                message.append(term)
                line = line - term
        message.append(jnp.zeros((10, 128), F32))
        buf2[q] = jnp.concatenate(message, axis=0).astype(BF16)
        to_all(buf2, q, y_send.at[layer], y_recv.at[layer], False)
        wait_all(buf2, y_recv.at[layer])
        if layer == 0:
            attn = merge(own_ids, stage2[0])
            own_state = own_state + dot(attn.astype(BF16), wop[0])

    attn = merge(all_ids, stage2[1])
    final = state[...] + dot(attn.astype(BF16), wop[1])
    mean = jnp.mean(final, axis=-1, keepdims=True)
    centered = final - mean
    var = jnp.mean(centered * centered, axis=-1, keepdims=True)
    embed = centered * lax.rsqrt(var + 1e-05) * gain_ref[...]
    state[...] = embed
    embed_ref[...] = state[pl.ds(pl.multiple_of(q * 8, 8), 8), :]
    mask_embed = dot(embed.astype(BF16), mw[...]).astype(BF16)
    logit_ref[...] = (dot_nt(mask_embed, pix[...]) * D**-0.5).astype(BF16)

    for copy in sends:
        copy.wait_send()
    wait_all(qbuf, q_send)
    for layer in range(LAYERS):
        wait_all(stage1.at[layer], s_send.at[layer])
        wait_all(stage2.at[layer], y_send.at[layer])


def local(
    features, conv_weight, queries, w_query, w_key, w_value, w_out, norm_gain, mask_weight, mask_blocks
):
    anywhere = pl.BlockSpec(memory_space=pl.ANY)
    vmem = pl.BlockSpec(memory_space=pltpu.VMEM)
    dma = pltpu.SemaphoreType.DMA
    square = pltpu.VMEM((LAYERS, D, D), BF16)
    embed, logits = pl.pallas_call(
        kernel,
        out_shape=(
            jax.ShapeDtypeStruct((8, D), F32),
            jax.ShapeDtypeStruct((NQ, 2 * NX), BF16),
        ),
        in_specs=[anywhere] * 7 + [vmem, anywhere, vmem],
        out_specs=(vmem, vmem),
        scratch_shapes=[
            pltpu.VMEM((3, 4, NX, D), BF16),
            pltpu.VMEM((3, 9, D, D), BF16),
            pltpu.VMEM((QRY, 8, D), F32),
            square,
            square,
            square,
            square,
            pltpu.VMEM((D, D), BF16),
            square,
            square,
            pltpu.VMEM((2 * NX, D), BF16),
            square,
            square,
            pltpu.VMEM((LAYERS, SPAN, 8, 128), F32),
            pltpu.VMEM((LAYERS, QRY, MSG, 128), BF16),
            pltpu.VMEM((NQ, D), F32),
            dma((7,)),
            dma((3,)),
            dma((8,)),
            dma((8,)),
            dma,
            dma,
            dma((LAYERS,)),
            dma((LAYERS,)),
            dma((LAYERS,)),
            dma((LAYERS,)),
        ],
        compiler_params=pltpu.CompilerParams(
            collective_id=0, has_side_effects=True, vmem_limit_bytes=40 * 1024 * 1024
        ),
    )(
        features,
        conv_weight.reshape(9, 3, D, D),
        queries,
        w_query,
        w_key,
        w_value,
        w_out,
        norm_gain.reshape(1, D),
        mask_weight,
        mask_blocks,
    )
    return embed, logits.reshape(NQ, 1, 2, NX)


def solution(mesh):
    return jax.shard_map(
        local,
        mesh=mesh,
        in_specs=(
            P("span", "qry", None, None),
            P(),
            P("qry", None),
            P(),
            P(),
            P(),
            P(),
            P(),
            P(),
            P(),
        ),
        out_specs=(P("qry", None), P(None, "span", "qry", None)),
        check_vma=False,
    )
```

time: 227 us -> 58.7 us (0.26); the launches traced: 224 us -> 58.3 us
  local copies, waits for them, and re-layouts: 80.7 us -> 11 us
  Pallas kernels: 0 us -> 46.7 us
  starting transfers between devices: 42.8 us -> 0 us
  waiting for transfers between devices: 36.6 us -> 0 us
  blocking collectives: 23.7 us -> 0 us
  other arithmetic: 20.5 us -> 0 us
  matrix products: 17.9 us -> 0 us
    pallas_call x0 -> x1, Pallas kernels: none -> 46.7 us  [local(): pl.pallas_call(kernel, out_shape=(jax.ShapeDtypeStruct((8, D), F32), jax....]
    all_to_all x5 -> x0, waiting for transfers between devices: 31.4 us -> none  [from_everyone(): lax.all_to_all(jnp.broadcast_to(x[None], (size, *x.shape)), axis, 0, 0, t...]
    all_to_all x5 -> x0, starting transfers between devices: 30.4 us -> none  [from_everyone(): lax.all_to_all(jnp.broadcast_to(x[None], (size, *x.shape)), axis, 0, 0, t...]
    all_to_all x2 -> x0, blocking collectives: 23.7 us -> none  [in_one_piece(): lax.all_to_all(both, axis, split_axis=split_dim, concat_axis=concat_dim,...]
    dot_general x26 -> x0, matrix products: 17.9 us -> none  [the longest x4 4.81 us: one_group(): jnp.einsum('nhe,vhe->nhv', group_q, partial_keys, preferred_element_type=...]
    dynamic_update_slice x12 -> x0, local copies, waits for them, and re-layouts: 17.5 us -> none  [local(): lax.map(one_group, (qproj, present_groups))]
    unnamed x123 -> x20, local copies, waits for them, and re-layouts: 26.1 us -> 10.4 us
    ppermute x4 -> x0, starting transfers between devices: 12.4 us -> none  [the longest x2 8.96 us: with_halo(): lax.ppermute(tail, axis, [(i, (i + 1) % count) for i in range(ends)])]
  transfers between devices with their start and end apart: 9 -> 0, of which waited for: 6 -> 0; matrix products, arithmetic and copies ran while one was open for 16% -> 0% of each run, Pallas kernels for 0% -> 0%
where the time goes in v1:
time: 58.7 us; the launch traced here: 58.3 us
  Pallas kernels  46.7 us (80%)
  local copies, waits for them, and re-layouts  11 us (19%)
  between operations  0.65 us (1%)
    pallas_call x1, Pallas kernels, local(): pl.pallas_call(kernel, out_shape=(jax.ShapeDtypeStruct((8, D), F32), jax....  46.7 us
    unnamed x20, local copies, waits for them, and re-layouts  10.4 us

profile of v1, /device:TPU:1, one launch (start us, length us, event | category | flops | bytes accessed | tf_op | source)
XLA Modules:
  0.0 58.3 jit_solution(11436304651062743792)
XLA Ops:
  0.6 0.8 %copy.12.mb_ref = s32[128,4]{1,0:T(8,128)S(1)} copy(s32[128,4]{0,1:T(4,128)} %param.19) | data formatting | bytes 4096 | tf_op args[9]
  1.4 0.0 copy-start
  1.4 2.0 %copy-done = bf16[27,256,256]{2,1,0:T(8,128)(2,1)S(1)} copy-done((bf16[27,256,256]{2,1,0:T(8,128)(2,1)S(1)}, bf16[27,256,256]{2,1,0:T(8,128)(2,1)}, u32[]{:S(2)}) %copy-start) | copy-done | bytes 3538968
  3.4 0.0 copy-start.1
  3.4 0.9 %copy-done.1 = bf16[2,256,256]{2,1,0:T(8,128)(2,1)S(1)} copy-done((bf16[2,256,256]{2,1,0:T(8,128)(2,1)S(1)}, bf16[2,256,256]{2,1,0:T(8,128)(2,1)}, u32[]{:S(2)}) %copy-start.1) | copy-done | bytes 262168
  4.4 0.0 copy-start.2
  4.4 0.9 %copy-done.2 = bf16[2,256,256]{2,1,0:T(8,128)(2,1)S(1)} copy-done((bf16[2,256,256]{2,1,0:T(8,128)(2,1)S(1)}, bf16[2,256,256]{2,1,0:T(8,128)(2,1)}, u32[]{:S(2)}) %copy-start.2) | copy-done | bytes 262168
  5.3 0.0 copy-start.3
  5.3 0.9 %copy-done.3 = bf16[2,256,256]{2,1,0:T(8,128)(2,1)S(1)} copy-done((bf16[2,256,256]{2,1,0:T(8,128)(2,1)S(1)}, bf16[2,256,256]{2,1,0:T(8,128)(2,1)}, u32[]{:S(2)}) %copy-start.3) | copy-done | bytes 262168
  6.3 0.0 copy-start.4
  6.3 0.9 %copy-done.4 = bf16[2,256,256]{2,1,0:T(8,128)(2,1)S(1)} copy-done((bf16[2,256,256]{2,1,0:T(8,128)(2,1)S(1)}, bf16[2,256,256]{2,1,0:T(8,128)(2,1)}, u32[]{:S(2)}) %copy-start.4) | copy-done | bytes 262168
  7.2 0.0 copy-start.5
  7.2 0.9 %copy-done.5 = bf16[1,2,128,256]{3,2,1,0:T(8,128)(2,1)S(1)} copy-done((bf16[1,2,128,256]{3,2,1,0:T(8,128)(2,1)S(1)}, bf16[1,2,128,256]{3,2,1,0:T(8,128)(2,1)}, u32[]{:S(2)}) %copy-start.5) | copy-done | bytes 131096
  8.1 0.0 copy-start.6
  8.1 0.9 %copy-done.6 = bf16[256,256]{1,0:T(8,128)(2,1)S(1)} copy-done((bf16[256,256]{1,0:T(8,128)(2,1)S(1)}, bf16[256,256]{1,0:T(8,128)(2,1)}, u32[]{:S(2)}) %copy-start.6) | copy-done | bytes 131096
  9.0 0.0 copy-start.7
  9.0 0.7 %copy-done.7 = f32[8,256]{1,0:T(8,128)S(1)} copy-done((f32[8,256]{1,0:T(8,128)S(1)}, f32[8,256]{1,0:T(8,128)}, u32[]{:S(2)}) %copy-start.7) | copy-done | bytes 8216
  9.7 0.0 copy-start.8
  9.7 0.7 %copy-done.8 = f32[256]{0:T(256)S(1)} copy-done((f32[256]{0:T(256)S(1)}, f32[256]{0:T(256)}, u32[]{:S(2)}) %copy-start.8) | copy-done | bytes 1048
  10.4 46.7 %shard_map.113 = (f32[8,256]{1,0:T(8,128)S(1)}, bf16[128,256]{1,0:T(8,128)(2,1)S(1)}) custom-call(bf16[1,2,128,256]{3,2,1,0:T(8,128)(2,1)S(1)} %copy-done.5, bf16[9,3,256,256]{3,2,1,0:T(8,128)(2,1)S(1)} %bitcast.3, f32[8,256]{1,0:T(8,128)S(1)} %copy-done.7, bf16[2,256,256]{2,1,0:T(8,128)(2,1)S(1)} %copy-done.1, bf16[2,256,256]{2,1,0:T(8,128)(2,1)S(1)} %copy-done.2, ...), custom_call_target="tpu_custom_call" | custom-call | tf_op jit(solution)/shard_map/pallas_call | solution.py:283
  57.1 0.7 %reshape.15 = bf16[128,1,2,128]{3,2,0,1:T(2,128)(2,1)} reshape(bf16[128,256]{1,0:T(8,128)(2,1)S(1)} %get-tuple-element.5) | data formatting | bytes 131072 | tf_op jit(solution)/shard_map/reshape | solution.py:334
  57.8 0.6 %copy.15 = f32[8,256]{1,0:T(8,128)} copy(f32[8,256]{1,0:T(8,128)S(1)} %get-tuple-element.10) | data formatting | bytes 16384
Async XLA Ops:
  1.4 2.0 %copy-start = (bf16[27,256,256]{2,1,0:T(8,128)(2,1)S(1)}, bf16[27,256,256]{2,1,0:T(8,128)(2,1)}, u32[]{:S(2)}) copy-start(bf16[27,256,256]{2,1,0:T(8,128)(2,1)} %param.11) | copy-start | bytes 10616836
  3.4 0.9 %copy-start.1 = (bf16[2,256,256]{2,1,0:T(8,128)(2,1)S(1)}, bf16[2,256,256]{2,1,0:T(8,128)(2,1)}, u32[]{:S(2)}) copy-start(bf16[2,256,256]{2,1,0:T(8,128)(2,1)} %wq_hbm.1) | copy-start | bytes 786436
  4.4 0.9 %copy-start.2 = (bf16[2,256,256]{2,1,0:T(8,128)(2,1)S(1)}, bf16[2,256,256]{2,1,0:T(8,128)(2,1)}, u32[]{:S(2)}) copy-start(bf16[2,256,256]{2,1,0:T(8,128)(2,1)} %wk_hbm.1) | copy-start | bytes 786436
  5.3 0.9 %copy-start.3 = (bf16[2,256,256]{2,1,0:T(8,128)(2,1)S(1)}, bf16[2,256,256]{2,1,0:T(8,128)(2,1)}, u32[]{:S(2)}) copy-start(bf16[2,256,256]{2,1,0:T(8,128)(2,1)} %wv_hbm.1) | copy-start | bytes 786436
  6.3 0.9 %copy-start.4 = (bf16[2,256,256]{2,1,0:T(8,128)(2,1)S(1)}, bf16[2,256,256]{2,1,0:T(8,128)(2,1)}, u32[]{:S(2)}) copy-start(bf16[2,256,256]{2,1,0:T(8,128)(2,1)} %wo_hbm.1) | copy-start | bytes 786436
  7.2 0.9 %copy-start.5 = (bf16[1,2,128,256]{3,2,1,0:T(8,128)(2,1)S(1)}, bf16[1,2,128,256]{3,2,1,0:T(8,128)(2,1)}, u32[]{:S(2)}) copy-start(bf16[1,2,128,256]{3,2,1,0:T(8,128)(2,1)} %feat_hbm.1) | copy-start | bytes 393220
  8.1 0.9 %copy-start.6 = (bf16[256,256]{1,0:T(8,128)(2,1)S(1)}, bf16[256,256]{1,0:T(8,128)(2,1)}, u32[]{:S(2)}) copy-start(bf16[256,256]{1,0:T(8,128)(2,1)} %mw_hbm.1) | copy-start | bytes 393220
  9.0 0.7 %copy-start.7 = (f32[8,256]{1,0:T(8,128)S(1)}, f32[8,256]{1,0:T(8,128)}, u32[]{:S(2)}) copy-start(f32[8,256]{1,0:T(8,128)} %queries_hbm.1) | copy-start | bytes 24580
  9.7 0.7 %copy-start.8 = (f32[256]{0:T(256)S(1)}, f32[256]{0:T(256)}, u32[]{:S(2)}) copy-start(f32[256]{0:T(256)} %param.17) | copy-start | bytes 3076

commit v2 on v1

v2 whole, which is shorter than its diff:
```python
import jax
import jax.numpy as jnp
from jax import lax
from jax.experimental import pallas as pl
from jax.experimental.pallas import tpu as pltpu
from jax.sharding import PartitionSpec as P

MESH = pl.DeviceIdType.MESH
HEADS = 8
LAYERS = 2
D = 256
HEAD_DIM = 32
NX = 128
NQ = 128
MB = 4
NY = 32
SPAN = 16
QRY = 16
F32 = jnp.float32
BF16 = jnp.bfloat16
ZS = 8
NEAR_ROWS = 32
FAR_ROWS = 48
Z_ORDER = (0, 1, 7, 2, 6, 3, 5, 4)
Z_SENDS = (4, 3, 5, 2, 6, 1, 7)
XY_SENDS = sorted(
    ((dy, dx) for dy in range(4) for dx in range(4) if dy or dx),
    key=lambda t: -(min(t[0], 4 - t[0]) + min(t[1], 4 - t[1])),
)


def iota(shape, dim):
    return lax.broadcasted_iota(jnp.int32, shape, dim)


def dot(a, b):
    return jnp.dot(a, b, preferred_element_type=F32)


def dot_nt(a, b):
    return lax.dot_general(a, b, (((1,), (1,)), ((), ())), preferred_element_type=F32)


def wrap(i, n):
    return lax.rem(i + n, n)


def slot_plane(slot, z):
    place = slot // 2
    offset = jnp.zeros_like(slot)
    for k, dz in enumerate(Z_ORDER):
        offset = jnp.where(place == k, dz, offset)
    return ((z + offset) % ZS) * 2 + slot % 2


def merge(ids, near, far, pair_id, term_y, lane_z):
    rows = ids.shape[0]
    outs = jnp.concatenate(
        [
            jnp.concatenate(
                [part[:, half * 16 : half * 16 + 16, :].reshape(QRY * 16, 128) for half in range(2)],
                axis=1,
            )
            for part in (near, far)
        ],
        axis=0,
    )
    terms = far[:, 32:FAR_ROWS, :].reshape(QRY * 16, 128)
    pick, term = [], []
    for j in range(MB):
        idj = ids[:, j : j + 1]
        pick.append(jnp.where(pair_id == idj, 1.0, 0.0).astype(BF16))
        term.append(jnp.where(term_y == idj % NY, 1.0, 0.0).astype(BF16))
    lse = dot(jnp.concatenate(term, axis=0), terms)
    chosen = dot(jnp.concatenate(pick, axis=0), outs)
    lses = []
    for j in range(MB):
        lj = jnp.where(lane_z == ids[:, j : j + 1] // NY, lse[j * rows : (j + 1) * rows], 0.0)
        for shift in (8, 16, 32, 64):
            lj = lj + pltpu.roll(lj, shift, axis=1)
        lses.append(lj)
    top = jnp.maximum(jnp.maximum(lses[0], lses[1]), jnp.maximum(lses[2], lses[3]))
    weights = [jnp.exp(lj - top) for lj in lses]
    inv = 1.0 / (weights[0] + weights[1] + weights[2] + weights[3])
    attn = jnp.zeros((rows, D), F32)
    for j in range(MB):
        wj = weights[j] * inv
        attn = attn + jnp.concatenate([wj, wj], axis=1) * chosen[j * rows : (j + 1) * rows]
    return attn


def kernel(
    feat_hbm, conv_hbm, queries_hbm, wq_hbm, wk_hbm, wv_hbm, wo_hbm, gain_hbm, mw_hbm, mb_hbm,
    embed_ref, logit_ref,
    ext, taps, qbuf, qpbuf, wq, wk, wv, wo, mw, gain, mb, wvp, wop, pix, keys, vals,
    stage1, near, far, state,
    local_sem, conv_sem, halo_send, halo_recv, q_send, q_recv, p_send, p_recv,
    s_send, s_recv, y_send, y_recv,
):
    s = lax.axis_index("span")
    q = lax.axis_index("qry")
    z, core = s // 2, lax.rem(s, 2)
    y, x = q // 4, lax.rem(q, 4)
    up, down = wrap(s + 1, SPAN), wrap(s - 1, SPAN)
    right, left = wrap(q + 1, QRY), wrap(q - 1, QRY)
    z_peers = [(d, c) for d in Z_SENDS for c in range(2)] + [(0, 1)]
    z_index = [wrap(z + d, ZS) * 2 + (c if d else 1 - core) for d, c in z_peers]
    xy_index = [lax.rem(y + dy, 4) * 4 + lax.rem(x + dx, 4) for dy, dx in XY_SENDS]

    barrier = pltpu.get_barrier_semaphore()
    for plane in z_index[::-1]:
        pl.semaphore_signal(barrier, inc=1, device_id=(plane, q), device_id_type=MESH)
    for block in xy_index[::-1]:
        pl.semaphore_signal(barrier, inc=1, device_id=(s, block), device_id_type=MESH)

    own = pltpu.make_async_copy(feat_hbm.at[0], ext.at[1, pl.ds(1, 2)], local_sem.at[0])
    own.start()
    early, loads = [], []
    for k, (src, dst) in enumerate(
        (
            (mb_hbm, mb),
            (queries_hbm, qbuf.at[q]),
            (wq_hbm, wq),
            (wv_hbm, wv),
            (wo_hbm, wo),
            (wk_hbm, wk),
            (mw_hbm, mw),
            (gain_hbm, gain),
        )
    ):
        copy = pltpu.make_async_copy(src, dst, local_sem.at[1 + k])
        copy.start()
        (early if k < 3 else loads).append(copy)
    conv_loads = [
        pltpu.make_async_copy(conv_hbm.at[:, dx], taps.at[dx], conv_sem.at[dx]) for dx in range(3)
    ]
    for load in conv_loads:
        load.start()
    pl.semaphore_wait(barrier, len(z_index) + len(xy_index))

    sends = []

    def send(src, dst, k, peer):
        copy = pltpu.make_async_remote_copy(
            src_ref=src, dst_ref=dst, send_sem=halo_send.at[k], recv_sem=halo_recv.at[k],
            device_id=peer, device_id_type=MESH,
        )
        copy.start()
        sends.append(copy)
        return copy

    rows = feat_hbm.at[0]
    from_left = send(rows.at[1], ext.at[1, 0], 0, (s, right))
    from_right = send(rows.at[0], ext.at[1, 3], 1, (s, left))
    from_down = send(rows, ext.at[0, pl.ds(1, 2)], 2, (up, q))
    from_up = send(rows, ext.at[2, pl.ds(1, 2)], 3, (down, q))

    def to_plane(buf, send_sem, recv_sem):
        for block in xy_index:
            pltpu.make_async_remote_copy(
                src_ref=buf.at[q], dst_ref=buf.at[q], send_sem=send_sem, recv_sem=recv_sem,
                device_id=(s, block), device_id_type=MESH,
            ).start()

    def wait_slots(buf, count, sem):
        some = buf.at[pl.ds(0, count)]
        pltpu.make_async_copy(some, some, sem).wait()

    for load in early:
        load.wait()
    qproj = (dot(qbuf[q].astype(BF16), wq[0]) * HEAD_DIM**-0.5).astype(BF16)
    qpbuf[q] = jnp.concatenate([qproj[:, 0:128], qproj[:, 128:256]], axis=0)
    to_plane(qpbuf, p_send, p_recv)

    perm = jnp.where(
        iota((D, D), 1) == (iota((D, D), 0) % HEAD_DIM) * HEADS + iota((D, D), 0) // HEAD_DIM, 1.0, 0.0
    ).astype(BF16)
    perm_t = jnp.where(
        iota((D, D), 0) == (iota((D, D), 1) % HEAD_DIM) * HEADS + iota((D, D), 1) // HEAD_DIM, 1.0, 0.0
    ).astype(BF16)
    for load in loads:
        load.wait()
    for layer in range(LAYERS):
        wvp[layer] = dot(wv[layer], perm).astype(BF16)
        wop[layer] = dot(perm_t, wo[layer]).astype(BF16)

    lists = mb[...]
    all_ids = lists.astype(F32).T.astype(jnp.int32)
    own_ids, picks, listed = [], [], []
    for r in range(2):
        block_id = s * NY + q * 2 + r
        listed.append(jnp.max(jnp.where(all_ids == block_id, 1, 0), axis=1, keepdims=True) > 0)
        picks.append(jnp.max(jnp.where(lists == block_id, 1.0, 0.0), axis=0, keepdims=True))
        own_ids.append(jnp.sum(jnp.where(listed[r], all_ids.astype(F32), 0.0), axis=0, keepdims=True))
    own_ids = jnp.concatenate(own_ids + [jnp.full((6, MB), -1.0, F32)], axis=0).astype(jnp.int32)
    picks = jnp.concatenate(picks + [jnp.zeros((6, NQ), F32)], axis=0).astype(BF16)

    col = iota((1, QRY * 32), 1)
    pair_id = slot_plane((col // 256) * 8 + col % 8, z) * NY + ((col % 256) // 16) * 2 + (col // 8) % 2
    row = iota((1, QRY * 16), 1)
    kind = row % 16
    term_y = jnp.where(kind < 6, (row // 16) * 2 + jnp.where(kind < 3, 0, 1), -1)
    lane_z = slot_plane(iota((1, 128), 1) // HEADS, z)

    from_left.wait_recv()
    send(ext.at[1, 0], ext.at[0, 0], 4, (up, q))
    send(ext.at[1, 0], ext.at[2, 0], 5, (down, q))
    from_right.wait_recv()
    send(ext.at[1, 3], ext.at[0, 3], 6, (up, q))
    send(ext.at[1, 3], ext.at[2, 3], 7, (down, q))
    own.wait()
    for load in conv_loads:
        load.wait()
    for copy in sends[2:]:
        copy.wait_recv()

    @pl.when(s == 0)
    def _():
        ext[0] = jnp.zeros((4, NX, D), BF16)

    @pl.when(s == SPAN - 1)
    def _():
        ext[2] = jnp.zeros((4, NX, D), BF16)

    for k in range(4, 8):
        sends[k].wait_send()

    @pl.when(q == 0)
    def _():
        ext[:, 0] = jnp.zeros((3, NX, D), BF16)

    @pl.when(q == QRY - 1)
    def _():
        ext[:, 3] = jnp.zeros((3, NX, D), BF16)

    slab = jnp.concatenate(
        [ext[dz, dy : dy + 2].reshape(2 * NX, D) for dz in range(3) for dy in range(3)], axis=1
    )
    x_at = iota((2 * NX, D), 0) % NX
    before = dot(slab, taps[0].reshape(9 * D, D))
    conv = jnp.where(x_at == 0, 0.0, pltpu.roll(before, 1, axis=0))
    conv = conv + dot(slab, taps[1].reshape(9 * D, D))
    after = dot(slab, taps[2].reshape(9 * D, D))
    conv = conv + jnp.where(x_at == NX - 1, 0.0, pltpu.roll(after, 2 * NX - 1, axis=0))
    pixel = jnp.maximum(conv, 0.0).astype(BF16)
    pix[...] = pixel
    keys[0] = dot(pixel, wk[0]).astype(BF16)
    vals[0] = dot(pixel, wvp[0]).astype(BF16)

    wait_slots(qpbuf, QRY - 1, p_recv)
    projected = jnp.concatenate(
        [qpbuf[:, half * 8 : half * 8 + 8, :].astype(F32).reshape(NQ, 128) for half in range(2)], axis=1
    )
    qproj = dot(picks, projected.astype(BF16))

    head_of = iota((HEADS, D), 1) // HEAD_DIM == iota((HEADS, D), 0)
    head_of_lane = iota((HEADS, D), 1) % HEADS == iota((HEADS, D), 0)
    lse_lane = iota((HEADS, 128), 1) % HEADS == iota((HEADS, 128), 0)
    own_slot = iota((HEADS, 128), 1) // HEADS
    for layer in range(LAYERS):
        spread = jnp.concatenate(
            [jnp.where(head_of, qproj[r : r + 1], 0.0) for r in range(2)], axis=0
        ).astype(BF16)
        scores = dot_nt(spread, keys[layer])
        scores = jnp.concatenate([scores[0:8, 0:NX], scores[8:16, NX : 2 * NX]], axis=0)
        top = jnp.max(scores, axis=1, keepdims=True)
        prob = jnp.exp(scores - top)
        total = jnp.sum(prob, axis=1, keepdims=True)
        inv = 1.0 / total
        lse = top + jnp.log(total)
        prob = prob.astype(BF16)
        low, high, lines = [], [], []
        for r in range(2):
            part = slice(r * HEADS, (r + 1) * HEADS)
            weighted = dot(prob[part], vals[layer, r * NX : (r + 1) * NX])
            out = jnp.sum(jnp.where(head_of_lane, weighted * inv[part], 0.0), axis=0, keepdims=True)
            low.append(out[:, 0:128])
            high.append(out[:, 128:256])
            lines.append(jnp.sum(jnp.where(lse_lane, lse[part], 0.0), axis=0, keepdims=True))
        buf = stage1.at[layer]
        buf[core] = jnp.concatenate(low + high + lines + [jnp.zeros((2, 128), F32)], axis=0)
        for (d, c), plane in zip(z_peers, z_index):
            place = Z_ORDER.index((ZS - d) % ZS)
            pltpu.make_async_remote_copy(
                src_ref=buf.at[core], dst_ref=buf.at[place * 2 + core],
                send_sem=s_send.at[layer], recv_sem=s_recv.at[layer, place // 4],
                device_id=(plane, q), device_id_type=MESH,
            ).start()
        if layer == 0:
            to_plane(qbuf, q_send, q_recv)
            keys[1] = dot(pix[...], wk[1]).astype(BF16)
            vals[1] = dot(pix[...], wvp[1]).astype(BF16)
        else:
            attn = merge(all_ids, near[0], far[0], pair_id, term_y, lane_z)
            state[...] = qbuf[...].reshape(NQ, D) + dot(attn.astype(BF16), wop[0])
        message, lines = [], []
        for group in range(2):
            wait_slots(buf, 7 + group, s_recv.at[layer, group])
            got = stage1[layer, group * 8 : group * 8 + 8]
            message = [got[:, k, :] for k in range(4)]
            lines.append(
                [
                    jnp.sum(
                        jnp.where(own_slot == group * 8 + iota((8, 128), 0), got[:, 4 + r, :], 0.0),
                        axis=0,
                        keepdims=True,
                    )
                    for r in range(2)
                ]
            )
            if group == 0:
                near[layer, q] = jnp.concatenate(message, axis=0).astype(BF16)
                to_plane(near.at[layer], y_send.at[layer, 0], y_recv.at[layer, 0])
        for r in range(2):
            line = lines[0][r] + lines[1][r]
            for _ in range(3):
                term = line.astype(BF16).astype(F32)
                message.append(term)
                line = line - term
        message.append(jnp.zeros((10, 128), F32))
        far[layer, q] = jnp.concatenate(message, axis=0).astype(BF16)
        to_plane(far.at[layer], y_send.at[layer, 1], y_recv.at[layer, 1])
        if layer == 0:
            wait_slots(qbuf, QRY - 1, q_recv)
            state_all = qbuf[...].reshape(NQ, D)
            own_state = [
                jnp.sum(jnp.where(listed[r], state_all, 0.0), axis=0, keepdims=True) for r in range(2)
            ]
            own_state = jnp.concatenate(own_state + [jnp.zeros((6, D), F32)], axis=0)
        wait_slots(near.at[layer], QRY - 1, y_recv.at[layer, 0])
        wait_slots(far.at[layer], QRY - 1, y_recv.at[layer, 1])
        if layer == 0:
            attn = merge(own_ids, near[0], far[0], pair_id, term_y, lane_z)
            own_state = own_state + dot(attn.astype(BF16), wop[0])
            qproj = (dot(own_state.astype(BF16), wq[1]) * HEAD_DIM**-0.5).astype(BF16).astype(F32)

    attn = merge(all_ids, near[1], far[1], pair_id, term_y, lane_z)
    final = state[...] + dot(attn.astype(BF16), wop[1])
    mean = jnp.mean(final, axis=-1, keepdims=True)
    centered = final - mean
    var = jnp.mean(centered * centered, axis=-1, keepdims=True)
    embed = centered * lax.rsqrt(var + 1e-05) * gain[...]
    state[...] = embed
    embed_ref[...] = state[pl.ds(pl.multiple_of(q * 8, 8), 8), :]
    mask_embed = dot(embed.astype(BF16), mw[...]).astype(BF16)
    logit_ref[...] = (dot_nt(mask_embed, pix[...]) * D**-0.5).astype(BF16)

    for copy in sends[:4]:
        copy.wait_send()
    wait_slots(qbuf, QRY - 1, q_send)
    wait_slots(qpbuf, QRY - 1, p_send)
    for layer in range(LAYERS):
        wait_slots(stage1.at[layer], SPAN - 1, s_send.at[layer])
        wait_slots(near.at[layer], QRY - 1, y_send.at[layer, 0])
        wait_slots(far.at[layer], QRY - 1, y_send.at[layer, 1])


def local(
    features, conv_weight, queries, w_query, w_key, w_value, w_out, norm_gain, mask_weight, mask_blocks
):
    hbm = pl.BlockSpec(memory_space=pltpu.HBM)
    vmem = pl.BlockSpec(memory_space=pltpu.VMEM)
    dma = pltpu.SemaphoreType.DMA
    square = pltpu.VMEM((LAYERS, D, D), BF16)
    embed, logits = pl.pallas_call(
        kernel,
        out_shape=(
            jax.ShapeDtypeStruct((8, D), F32),
            jax.ShapeDtypeStruct((NQ, 2 * NX), BF16),
        ),
        in_specs=[hbm] * 10,
        out_specs=(vmem, vmem),
        scratch_shapes=[
            pltpu.VMEM((3, 4, NX, D), BF16),
            pltpu.VMEM((3, 9, D, D), BF16),
            pltpu.VMEM((QRY, 8, D), F32),
            pltpu.VMEM((QRY, 16, 128), BF16),
            square,
            square,
            square,
            square,
            pltpu.VMEM((D, D), BF16),
            pltpu.VMEM((1, D), F32),
            pltpu.VMEM((MB, NQ), jnp.int32),
            square,
            square,
            pltpu.VMEM((2 * NX, D), BF16),
            square,
            square,
            pltpu.VMEM((LAYERS, SPAN, 8, 128), F32),
            pltpu.VMEM((LAYERS, QRY, NEAR_ROWS, 128), BF16),
            pltpu.VMEM((LAYERS, QRY, FAR_ROWS, 128), BF16),
            pltpu.VMEM((NQ, D), F32),
            dma((9,)),
            dma((3,)),
            dma((8,)),
            dma((8,)),
            dma,
            dma,
            dma,
            dma,
            dma((LAYERS,)),
            dma((LAYERS, 2)),
            dma((LAYERS, 2)),
            dma((LAYERS, 2)),
        ],
        compiler_params=pltpu.CompilerParams(
            collective_id=0, has_side_effects=True, vmem_limit_bytes=60 * 1024 * 1024
        ),
    )(
        features,
        conv_weight.reshape(9, 3, D, D),
        queries,
        w_query,
        w_key,
        w_value,
        w_out,
        norm_gain.reshape(1, D),
        mask_weight,
        mask_blocks.T,
    )
    return embed, logits.reshape(NQ, 1, 2, NX)


def solution(mesh):
    return jax.shard_map(
        local,
        mesh=mesh,
        in_specs=(
            P("span", "qry", None, None),
            P(),
            P("qry", None),
            P(),
            P(),
            P(),
            P(),
            P(),
            P(),
            P(),
        ),
        out_specs=(P("qry", None), P(None, "span", "qry", None)),
        check_vma=False,
    )
```

time: 58.7 us -> 48.9 us (0.83)
  local copies, waits for them, and re-layouts: 11 us -> 2.78 us
  Pallas kernels: 46.7 us -> 45.3 us
    unnamed x20 -> x1, local copies, waits for them, and re-layouts: 10.4 us -> 1.29 us
    pallas_call x1, Pallas kernels: 46.7 us -> 45.3 us  [local(): pl.pallas_call(kernel, out_shape=(jax.ShapeDtypeStruct((8, D), F32), jax....]
    reshape x1, local copies, waits for them, and re-layouts: 0.65 us -> 1.49 us  [local(): return (embed, logits.reshape(NQ, 1, 2, NX))]
where the time goes in v2:
time: 48.9 us; the launch traced here: 48.8 us
  Pallas kernels  45.3 us (93%)
  local copies, waits for them, and re-layouts  2.78 us (6%)
  between operations  0.64 us (1%)
    pallas_call x1, Pallas kernels, local(): pl.pallas_call(kernel, out_shape=(jax.ShapeDtypeStruct((8, D), F32), jax....  45.3 us
    reshape x1, local copies, waits for them, and re-layouts, local(): return (embed, logits.reshape(NQ, 1, 2, NX))  1.49 us
    unnamed x1, local copies, waits for them, and re-layouts  1.29 us

profile of v2, /device:TPU:1, one launch (start us, length us, event | category | flops | bytes accessed | tf_op | source)
XLA Modules:
  0.0 48.8 jit_solution(16480335335243802300)
XLA Ops:
  0.6 45.3 %shard_map.113 = (f32[8,256]{1,0:T(8,128)}, bf16[128,256]{1,0:T(8,128)(2,1)}) custom-call(bf16[1,2,128,256]{3,2,1,0:T(8,128)(2,1)} %feat_hbm.1, bf16[9,3,256,256]{3,2,1,0:T(8,128)(2,1)} %bitcast.4, f32[8,256]{1,0:T(8,128)} %queries_hbm.1, bf16[2,256,256]{2,1,0:T(8,128)(2,1)} %wq_hbm.1, bf16[2,256,256]{2,1,0:T(8,128)(2,1)} %wk_hbm.1, ...), custom_call_target="tpu_custom_call" | custom-call | tf_op jit(solution)/shard_map/pallas_call | solution.py:365
  46.0 1.5 %reshape.15 = bf16[128,1,2,128]{3,2,0,1:T(2,128)(2,1)} reshape(bf16[128,256]{1,0:T(8,128)(2,1)} %get-tuple-element.5) | data formatting | bytes 131072 | tf_op jit(solution)/shard_map/reshape | solution.py:422
  47.5 1.3 %copy.14 = f32[8,256]{1,0:T(8,128)} copy(f32[8,256]{1,0:T(8,128)} %get-tuple-element.10) | data formatting | bytes 16384

commit v3 on v2

--- a/solution.py
+++ b/solution.py
@@ -19,6 +19,7 @@
 F32 = jnp.float32
 BF16 = jnp.bfloat16
 ZS = 8
+CHUNKS = 4
 NEAR_ROWS = 32
 FAR_ROWS = 48
 Z_ORDER = (0, 1, 7, 2, 6, 3, 5, 4)
@@ -93,7 +94,7 @@
     feat_hbm, conv_hbm, queries_hbm, wq_hbm, wk_hbm, wv_hbm, wo_hbm, gain_hbm, mw_hbm, mb_hbm,
     embed_ref, logit_ref,
     ext, taps, qbuf, qpbuf, wq, wk, wv, wo, mw, gain, mb, wvp, wop, pix, keys, vals,
-    stage1, near, far, state,
+    stage1, near, far, state, acc,
     local_sem, conv_sem, halo_send, halo_recv, q_send, q_recv, p_send, p_recv,
     s_send, s_recv, y_send, y_recv,
 ):
@@ -150,10 +151,13 @@
         return copy
 
     rows = feat_hbm.at[0]
-    from_left = send(rows.at[1], ext.at[1, 0], 0, (s, right))
-    from_right = send(rows.at[0], ext.at[1, 3], 1, (s, left))
-    from_down = send(rows, ext.at[0, pl.ds(1, 2)], 2, (up, q))
-    from_up = send(rows, ext.at[2, pl.ds(1, 2)], 3, (down, q))
+    chunks = [pl.ds(k * (NX // CHUNKS), NX // CHUNKS) for k in range(CHUNKS)]
+    across = []
+    for k, chunk in enumerate(chunks):
+        across.append(send(rows.at[1, chunk], ext.at[1, 0, chunk], 2 * k, (s, right)))
+        across.append(send(rows.at[0, chunk], ext.at[1, 3, chunk], 2 * k + 1, (s, left)))
+    from_down = send(rows, ext.at[0, pl.ds(1, 2)], 2 * CHUNKS, (up, q))
+    from_up = send(rows, ext.at[2, pl.ds(1, 2)], 2 * CHUNKS + 1, (down, q))
 
     def to_plane(buf, send_sem, recv_sem):
         for block in xy_index:
@@ -202,46 +206,69 @@
     term_y = jnp.where(kind < 6, (row // 16) * 2 + jnp.where(kind < 3, 0, 1), -1)
     lane_z = slot_plane(iota((1, 128), 1) // HEADS, z)
 
-    from_left.wait_recv()
-    send(ext.at[1, 0], ext.at[0, 0], 4, (up, q))
-    send(ext.at[1, 0], ext.at[2, 0], 5, (down, q))
-    from_right.wait_recv()
-    send(ext.at[1, 3], ext.at[0, 3], 6, (up, q))
-    send(ext.at[1, 3], ext.at[2, 3], 7, (down, q))
+    relays = []
+    for k, copy in enumerate(across):
+        copy.wait_recv()
+        chunk, row = chunks[k // 2], 3 * (k % 2)
+        first = 2 * CHUNKS + 2 + 2 * k
+        relays.append(send(ext.at[1, row, chunk], ext.at[0, row, chunk], first, (up, q)))
+        relays.append(send(ext.at[1, row, chunk], ext.at[2, row, chunk], first + 1, (down, q)))
     own.wait()
     for load in conv_loads:
         load.wait()
-    for copy in sends[2:]:
+
+    middle = [ext[1, row] for row in range(4)]
+    middle[0] = jnp.where(q > 0, middle[0], jnp.zeros_like(middle[0]))
+    middle[3] = jnp.where(q < QRY - 1, middle[3], jnp.zeros_like(middle[3]))
+    slab = jnp.concatenate(
+        [jnp.concatenate(middle[dy : dy + 2], axis=0) for dy in range(3)], axis=1
+    )
+    for dx in range(3):
+        acc[dx] = dot(slab, taps[dx, 3:6].reshape(3 * D, D))
+    for dz, copy, outside in ((0, from_down, s == 0), (2, from_up, s == SPAN - 1)):
         copy.wait_recv()
 
-    @pl.when(s == 0)
+        @pl.when(outside)
+        def _():
+            ext[dz, 1:3] = jnp.zeros((2, NX, D), BF16)
+
+        pair = jnp.concatenate([ext[dz, 1], ext[dz, 2]], axis=1)
+        for dx in range(3):
+            for r in range(2):
+                weights = taps[dx, 3 * dz + 1 - r : 3 * dz + 3 - r].reshape(2 * D, D)
+                acc[dx, r * NX : (r + 1) * NX] += dot(pair, weights)
+
+    for copy in relays:
+        copy.wait_recv()
+
+    @pl.when((s == 0) | (q == 0))
     def _():
-        ext[0] = jnp.zeros((4, NX, D), BF16)
-
-    @pl.when(s == SPAN - 1)
+        ext[0, 0] = jnp.zeros((NX, D), BF16)
+
+    @pl.when((s == 0) | (q == QRY - 1))
     def _():
-        ext[2] = jnp.zeros((4, NX, D), BF16)
-
-    for k in range(4, 8):
-        sends[k].wait_send()
-
-    @pl.when(q == 0)
+        ext[0, 3] = jnp.zeros((NX, D), BF16)
+
+    @pl.when((s == SPAN - 1) | (q == 0))
     def _():
-        ext[:, 0] = jnp.zeros((3, NX, D), BF16)
-
-    @pl.when(q == QRY - 1)
+        ext[2, 0] = jnp.zeros((NX, D), BF16)
+
+    @pl.when((s == SPAN - 1) | (q == QRY - 1))
     def _():
-        ext[:, 3] = jnp.zeros((3, NX, D), BF16)
-
-    slab = jnp.concatenate(
-        [ext[dz, dy : dy + 2].reshape(2 * NX, D) for dz in range(3) for dy in range(3)], axis=1
-    )
+        ext[2, 3] = jnp.zeros((NX, D), BF16)
+
+    def column(dx):
+        parts = []
+        for r in range(2):
+            corner = jnp.concatenate([ext[0, 3 * r], ext[2, 3 * r]], axis=1)
+            weights = jnp.concatenate([taps[dx, 2 * r], taps[dx, 6 + 2 * r]], axis=0)
+            parts.append(acc[dx, r * NX : (r + 1) * NX] + dot(corner, weights))
+        return jnp.concatenate(parts, axis=0)
+
     x_at = iota((2 * NX, D), 0) % NX
-    before = dot(slab, taps[0].reshape(9 * D, D))
-    conv = jnp.where(x_at == 0, 0.0, pltpu.roll(before, 1, axis=0))
-    conv = conv + dot(slab, taps[1].reshape(9 * D, D))
-    after = dot(slab, taps[2].reshape(9 * D, D))
-    conv = conv + jnp.where(x_at == NX - 1, 0.0, pltpu.roll(after, 2 * NX - 1, axis=0))
+    conv = jnp.where(x_at == 0, 0.0, pltpu.roll(column(0), 1, axis=0))
+    conv = conv + column(1)
+    conv = conv + jnp.where(x_at == NX - 1, 0.0, pltpu.roll(column(2), 2 * NX - 1, axis=0))
     pixel = jnp.maximum(conv, 0.0).astype(BF16)
     pix[...] = pixel
     keys[0] = dot(pixel, wk[0]).astype(BF16)
@@ -345,7 +372,7 @@
     mask_embed = dot(embed.astype(BF16), mw[...]).astype(BF16)
     logit_ref[...] = (dot_nt(mask_embed, pix[...]) * D**-0.5).astype(BF16)
 
-    for copy in sends[:4]:
+    for copy in sends:
         copy.wait_send()
     wait_slots(qbuf, QRY - 1, q_send)
     wait_slots(qpbuf, QRY - 1, p_send)
@@ -391,10 +418,11 @@
             pltpu.VMEM((LAYERS, QRY, NEAR_ROWS, 128), BF16),
             pltpu.VMEM((LAYERS, QRY, FAR_ROWS, 128), BF16),
             pltpu.VMEM((NQ, D), F32),
+            pltpu.VMEM((3, 2 * NX, D), F32),
             dma((9,)),
             dma((3,)),
-            dma((8,)),
-            dma((8,)),
+            dma((6 * CHUNKS + 2,)),
+            dma((6 * CHUNKS + 2,)),
             dma,
             dma,
             dma,

time: 48.9 us -> 47.2 us (0.965)
  Pallas kernels: 45.3 us -> 43.6 us
    pallas_call x1, Pallas kernels: 45.3 us -> 43.6 us  [local(): pl.pallas_call(kernel, out_shape=(jax.ShapeDtypeStruct((8, D), F32), jax....]
where the time goes in v3:
time: 47.2 us; the launch traced here: 47 us
  Pallas kernels  43.6 us (92%)
  local copies, waits for them, and re-layouts  2.78 us (6%)
  between operations  0.64 us (1%)
    pallas_call x1, Pallas kernels, local(): pl.pallas_call(kernel, out_shape=(jax.ShapeDtypeStruct((8, D), F32), jax....  43.6 us
    reshape x1, local copies, waits for them, and re-layouts, local(): return (embed, logits.reshape(NQ, 1, 2, NX))  1.49 us
    unnamed x1, local copies, waits for them, and re-layouts  1.29 us

profile of v3, /device:TPU:1, one launch (start us, length us, event | category | flops | bytes accessed | tf_op | source)
XLA Modules:
  0.0 47.0 jit_solution(12388770830010096504)
XLA Ops:
  0.6 43.6 %shard_map.113 = (f32[8,256]{1,0:T(8,128)}, bf16[128,256]{1,0:T(8,128)(2,1)}) custom-call(bf16[1,2,128,256]{3,2,1,0:T(8,128)(2,1)} %feat_hbm.1, bf16[9,3,256,256]{3,2,1,0:T(8,128)(2,1)} %bitcast.4, f32[8,256]{1,0:T(8,128)} %queries_hbm.1, bf16[2,256,256]{2,1,0:T(8,128)(2,1)} %wq_hbm.1, bf16[2,256,256]{2,1,0:T(8,128)(2,1)} %wk_hbm.1, ...), custom_call_target="tpu_custom_call" | custom-call | tf_op jit(solution)/shard_map/pallas_call | solution.py:392
  44.2 1.5 %reshape.15 = bf16[128,1,2,128]{3,2,0,1:T(2,128)(2,1)} reshape(bf16[128,256]{1,0:T(8,128)(2,1)} %get-tuple-element.5) | data formatting | bytes 131072 | tf_op jit(solution)/shard_map/reshape | solution.py:450
  45.7 1.3 %copy.14 = f32[8,256]{1,0:T(8,128)} copy(f32[8,256]{1,0:T(8,128)} %get-tuple-element.10) | data formatting | bytes 16384

commit v4 on v3

--- a/solution.py
+++ b/solution.py
@@ -20,9 +20,9 @@
 BF16 = jnp.bfloat16
 ZS = 8
 CHUNKS = 4
-NEAR_ROWS = 32
-FAR_ROWS = 48
 Z_ORDER = (0, 1, 7, 2, 6, 3, 5, 4)
+GROUPS = ((0, 8), (8, 14), (14, 16))
+PLACE_GROUP = (0, 0, 0, 0, 1, 1, 1, 2)
 Z_SENDS = (4, 3, 5, 2, 6, 1, 7)
 XY_SENDS = sorted(
     ((dy, dx) for dy in range(4) for dx in range(4) if dy or dx),
@@ -54,25 +54,27 @@
     return ((z + offset) % ZS) * 2 + slot % 2
 
 
-def merge(ids, near, far, pair_id, term_y, lane_z):
+def merge(ids, near, mid, far, pair_id, term_y, lane_z):
     rows = ids.shape[0]
+    flat = far.reshape(QRY * 16, 128)
+    raised = pltpu.roll(flat.astype(F32), QRY * 16 - 4, axis=0).astype(BF16)
     outs = jnp.concatenate(
         [
+            jnp.concatenate([near[half].reshape(QRY * 16, 128) for half in range(2)], axis=1),
             jnp.concatenate(
-                [part[:, half * 16 : half * 16 + 16, :].reshape(QRY * 16, 128) for half in range(2)],
+                [mid[:, half * 16 : half * 16 + 16, :].reshape(QRY * 16, 128) for half in range(2)],
                 axis=1,
-            )
-            for part in (near, far)
+            ),
+            jnp.concatenate([flat, raised], axis=1),
         ],
         axis=0,
     )
-    terms = far[:, 32:FAR_ROWS, :].reshape(QRY * 16, 128)
     pick, term = [], []
     for j in range(MB):
         idj = ids[:, j : j + 1]
         pick.append(jnp.where(pair_id == idj, 1.0, 0.0).astype(BF16))
         term.append(jnp.where(term_y == idj % NY, 1.0, 0.0).astype(BF16))
-    lse = dot(jnp.concatenate(term, axis=0), terms)
+    lse = dot(jnp.concatenate(term, axis=0), flat)
     chosen = dot(jnp.concatenate(pick, axis=0), outs)
     lses = []
     for j in range(MB):
@@ -94,9 +96,9 @@
     feat_hbm, conv_hbm, queries_hbm, wq_hbm, wk_hbm, wv_hbm, wo_hbm, gain_hbm, mw_hbm, mb_hbm,
     embed_ref, logit_ref,
     ext, taps, qbuf, qpbuf, wq, wk, wv, wo, mw, gain, mb, wvp, wop, pix, keys, vals,
-    stage1, near, far, state, acc,
+    stage1, near, mid, far, state, acc,
     local_sem, conv_sem, halo_send, halo_recv, q_send, q_recv, p_send, p_recv,
-    s_send, s_recv, y_send, y_recv,
+    s_send, s_recv, y_send, y_recv, c_send, c_recv, entered,
 ):
     s = lax.axis_index("span")
     q = lax.axis_index("qry")
@@ -109,8 +111,8 @@
     xy_index = [lax.rem(y + dy, 4) * 4 + lax.rem(x + dx, 4) for dy, dx in XY_SENDS]
 
     barrier = pltpu.get_barrier_semaphore()
-    for plane in z_index[::-1]:
-        pl.semaphore_signal(barrier, inc=1, device_id=(plane, q), device_id_type=MESH)
+    for d in (1, -1, 2, -2):
+        pl.semaphore_signal(barrier, inc=1, device_id=(wrap(s + d, SPAN), q), device_id_type=MESH)
     for block in xy_index[::-1]:
         pl.semaphore_signal(barrier, inc=1, device_id=(s, block), device_id_type=MESH)
 
@@ -137,7 +139,17 @@
     ]
     for load in conv_loads:
         load.start()
-    pl.semaphore_wait(barrier, len(z_index) + len(xy_index))
+    pl.semaphore_wait(barrier, 4 + len(xy_index))
+
+    def tell(step):
+        for k, d in enumerate((2 * step, -2 * step)):
+            pl.semaphore_signal(
+                entered.at[step - 1, k], inc=1, device_id=(wrap(s + d, SPAN), q), device_id_type=MESH
+            )
+
+    def hear(step):
+        for k in range(2):
+            pl.semaphore_wait(entered.at[step - 1, k], 1)
 
     sends = []
 
@@ -158,6 +170,8 @@
         across.append(send(rows.at[0, chunk], ext.at[1, 3, chunk], 2 * k + 1, (s, left)))
     from_down = send(rows, ext.at[0, pl.ds(1, 2)], 2 * CHUNKS, (up, q))
     from_up = send(rows, ext.at[2, pl.ds(1, 2)], 2 * CHUNKS + 1, (down, q))
+
+    tell(1)
 
     def to_plane(buf, send_sem, recv_sem):
         for block in xy_index:
@@ -199,11 +213,17 @@
     own_ids = jnp.concatenate(own_ids + [jnp.full((6, MB), -1.0, F32)], axis=0).astype(jnp.int32)
     picks = jnp.concatenate(picks + [jnp.zeros((6, NQ), F32)], axis=0).astype(BF16)
 
-    col = iota((1, QRY * 32), 1)
-    pair_id = slot_plane((col // 256) * 8 + col % 8, z) * NY + ((col % 256) // 16) * 2 + (col // 8) % 2
+    col = iota((1, QRY * 48), 1)
+    group, kind = col // 256, col % 16
+    slot = jnp.where(group < 2, group * 8 + col % 8, 14 + col % 2)
+    half = jnp.where(group < 2, kind // 8, kind // 2)
+    limit = jnp.where(group == 0, 8, jnp.where(group == 1, 6, 4))
+    pair_id = slot_plane(slot, z) * NY + ((col % 256) // 16) * 2 + half
+    pair_id = jnp.where(jnp.where(group < 2, col % 8, kind) < limit, pair_id, -2)
     row = iota((1, QRY * 16), 1)
-    kind = row % 16
-    term_y = jnp.where(kind < 6, (row // 16) * 2 + jnp.where(kind < 3, 0, 1), -1)
+    kind = row % 16 - 8
+    term_y = (row // 16) * 2 + jnp.where(kind < 3, 0, 1)
+    term_y = jnp.where((kind >= 0) & (kind < 6), term_y, -2)
     lane_z = slot_plane(iota((1, 128), 1) // HEADS, z)
 
     relays = []
@@ -213,6 +233,8 @@
         first = 2 * CHUNKS + 2 + 2 * k
         relays.append(send(ext.at[1, row, chunk], ext.at[0, row, chunk], first, (up, q)))
         relays.append(send(ext.at[1, row, chunk], ext.at[2, row, chunk], first + 1, (down, q)))
+    hear(1)
+    tell(2)
     own.wait()
     for load in conv_loads:
         load.wait()
@@ -283,7 +305,7 @@
     head_of = iota((HEADS, D), 1) // HEAD_DIM == iota((HEADS, D), 0)
     head_of_lane = iota((HEADS, D), 1) % HEADS == iota((HEADS, D), 0)
     lse_lane = iota((HEADS, 128), 1) % HEADS == iota((HEADS, 128), 0)
-    own_slot = iota((HEADS, 128), 1) // HEADS
+    hear(2)
     for layer in range(LAYERS):
         spread = jnp.concatenate(
             [jnp.where(head_of, qproj[r : r + 1], 0.0) for r in range(2)], axis=0
@@ -310,7 +332,7 @@
             place = Z_ORDER.index((ZS - d) % ZS)
             pltpu.make_async_remote_copy(
                 src_ref=buf.at[core], dst_ref=buf.at[place * 2 + core],
-                send_sem=s_send.at[layer], recv_sem=s_recv.at[layer, place // 4],
+                send_sem=s_send.at[layer], recv_sem=s_recv.at[layer, PLACE_GROUP[place]],
                 device_id=(plane, q), device_id_type=MESH,
             ).start()
         if layer == 0:
@@ -318,35 +340,36 @@
             keys[1] = dot(pix[...], wk[1]).astype(BF16)
             vals[1] = dot(pix[...], wvp[1]).astype(BF16)
         else:
-            attn = merge(all_ids, near[0], far[0], pair_id, term_y, lane_z)
+            attn = merge(all_ids, near[0], mid[0], far[0], pair_id, term_y, lane_z)
             state[...] = qbuf[...].reshape(NQ, D) + dot(attn.astype(BF16), wop[0])
-        message, lines = [], []
-        for group in range(2):
-            wait_slots(buf, 7 + group, s_recv.at[layer, group])
-            got = stage1[layer, group * 8 : group * 8 + 8]
-            message = [got[:, k, :] for k in range(4)]
-            lines.append(
-                [
-                    jnp.sum(
-                        jnp.where(own_slot == group * 8 + iota((8, 128), 0), got[:, 4 + r, :], 0.0),
-                        axis=0,
-                        keepdims=True,
-                    )
-                    for r in range(2)
-                ]
-            )
+        lines = [jnp.zeros((1, 128), F32)] * 2
+        for group, (start, end) in enumerate(GROUPS):
+            count = end - start
+            wait_slots(buf, count - (group == 0), s_recv.at[layer, group])
+            got = stage1[layer, start:end]
+            parts = [got[:, k, :] for k in range(4)]
+            own_lanes = iota((count, 128), 1) // HEADS == start + iota((count, 128), 0)
+            for r in range(2):
+                kept = jnp.where(own_lanes, got[:, 4 + r, :], 0.0)
+                lines[r] = lines[r] + jnp.sum(kept, axis=0, keepdims=True)
             if group == 0:
-                near[layer, q] = jnp.concatenate(message, axis=0).astype(BF16)
-                to_plane(near.at[layer], y_send.at[layer, 0], y_recv.at[layer, 0])
-        for r in range(2):
-            line = lines[0][r] + lines[1][r]
+                halves = [jnp.concatenate(parts[2 * k : 2 * k + 2], axis=0) for k in range(2)]
+                near[layer, core, q] = jnp.where(core == 0, halves[0], halves[1]).astype(BF16)
+                to_plane(near.at[layer, core], y_send.at[layer, 0], y_recv.at[layer, 0])
+            elif group == 1:
+                blank = jnp.zeros((2, 128), F32)
+                message = [piece for part in parts for piece in (part, blank)]
+                mid[layer, q] = jnp.concatenate(message, axis=0).astype(BF16)
+                to_plane(mid.at[layer], y_send.at[layer, 1], y_recv.at[layer, 1])
+        message = parts
+        for line in lines:
             for _ in range(3):
                 term = line.astype(BF16).astype(F32)
                 message.append(term)
                 line = line - term
-        message.append(jnp.zeros((10, 128), F32))
+        message.append(jnp.zeros((2, 128), F32))
         far[layer, q] = jnp.concatenate(message, axis=0).astype(BF16)
-        to_plane(far.at[layer], y_send.at[layer, 1], y_recv.at[layer, 1])
+        to_plane(far.at[layer], y_send.at[layer, 2], y_recv.at[layer, 2])
         if layer == 0:
             wait_slots(qbuf, QRY - 1, q_recv)
             state_all = qbuf[...].reshape(NQ, D)
@@ -354,14 +377,23 @@
                 jnp.sum(jnp.where(listed[r], state_all, 0.0), axis=0, keepdims=True) for r in range(2)
             ]
             own_state = jnp.concatenate(own_state + [jnp.zeros((6, D), F32)], axis=0)
-        wait_slots(near.at[layer], QRY - 1, y_recv.at[layer, 0])
-        wait_slots(far.at[layer], QRY - 1, y_recv.at[layer, 1])
+        wait_slots(near.at[layer, 0], QRY - 1, y_recv.at[layer, 0])
+        swap = pltpu.make_async_remote_copy(
+            src_ref=near.at[layer, core], dst_ref=near.at[layer, core],
+            send_sem=c_send.at[layer], recv_sem=c_recv.at[layer],
+            device_id=(z * 2 + 1 - core, q), device_id_type=MESH,
+        )
+        swap.start()
+        sends.append(swap)
+        wait_slots(mid.at[layer], QRY - 1, y_recv.at[layer, 1])
+        wait_slots(far.at[layer], QRY - 1, y_recv.at[layer, 2])
+        swap.wait_recv()
         if layer == 0:
-            attn = merge(own_ids, near[0], far[0], pair_id, term_y, lane_z)
+            attn = merge(own_ids, near[0], mid[0], far[0], pair_id, term_y, lane_z)
             own_state = own_state + dot(attn.astype(BF16), wop[0])
             qproj = (dot(own_state.astype(BF16), wq[1]) * HEAD_DIM**-0.5).astype(BF16).astype(F32)
 
-    attn = merge(all_ids, near[1], far[1], pair_id, term_y, lane_z)
+    attn = merge(all_ids, near[1], mid[1], far[1], pair_id, term_y, lane_z)
     final = state[...] + dot(attn.astype(BF16), wop[1])
     mean = jnp.mean(final, axis=-1, keepdims=True)
     centered = final - mean
@@ -378,8 +410,9 @@
     wait_slots(qpbuf, QRY - 1, p_send)
     for layer in range(LAYERS):
         wait_slots(stage1.at[layer], SPAN - 1, s_send.at[layer])
-        wait_slots(near.at[layer], QRY - 1, y_send.at[layer, 0])
-        wait_slots(far.at[layer], QRY - 1, y_send.at[layer, 1])
+        wait_slots(near.at[layer, 0], QRY - 1, y_send.at[layer, 0])
+        wait_slots(mid.at[layer], QRY - 1, y_send.at[layer, 1])
+        wait_slots(far.at[layer], QRY - 1, y_send.at[layer, 2])
 
 
 def local(
@@ -415,8 +448,9 @@
             square,
             square,
             pltpu.VMEM((LAYERS, SPAN, 8, 128), F32),
-            pltpu.VMEM((LAYERS, QRY, NEAR_ROWS, 128), BF16),
-            pltpu.VMEM((LAYERS, QRY, FAR_ROWS, 128), BF16),
+            pltpu.VMEM((LAYERS, 2, QRY, 16, 128), BF16),
+            pltpu.VMEM((LAYERS, QRY, 32, 128), BF16),
+            pltpu.VMEM((LAYERS, QRY, 16, 128), BF16),
             pltpu.VMEM((NQ, D), F32),
             pltpu.VMEM((3, 2 * NX, D), F32),
             dma((9,)),
@@ -428,9 +462,12 @@
             dma,
             dma,
             dma((LAYERS,)),
-            dma((LAYERS, 2)),
-            dma((LAYERS, 2)),
-            dma((LAYERS, 2)),
+            dma((LAYERS, 3)),
+            dma((LAYERS, 3)),
+            dma((LAYERS, 3)),
+            dma((LAYERS,)),
+            dma((LAYERS,)),
+            pltpu.SemaphoreType.REGULAR((2, 2)),
         ],
         compiler_params=pltpu.CompilerParams(
             collective_id=0, has_side_effects=True, vmem_limit_bytes=60 * 1024 * 1024

time: 47.2 us -> 46.6 us (0.987)
  Pallas kernels: 43.6 us -> 43 us
    pallas_call x1, Pallas kernels: 43.6 us -> 43 us  [local(): pl.pallas_call(kernel, out_shape=(jax.ShapeDtypeStruct((8, D), F32), jax....]
where the time goes in v4:
time: 46.6 us; the launch traced here: 46.5 us
  Pallas kernels  43 us (92%)
  local copies, waits for them, and re-layouts  2.78 us (6%)
  between operations  0.64 us (1%)
    pallas_call x1, Pallas kernels, local(): pl.pallas_call(kernel, out_shape=(jax.ShapeDtypeStruct((8, D), F32), jax....  43 us
    reshape x1, local copies, waits for them, and re-layouts, local(): return (embed, logits.reshape(NQ, 1, 2, NX))  1.49 us
    unnamed x1, local copies, waits for them, and re-layouts  1.29 us

profile of v4, /device:TPU:1, one launch (start us, length us, event | category | flops | bytes accessed | tf_op | source)
XLA Modules:
  0.0 46.5 jit_solution(14657789334409543435)
XLA Ops:
  0.6 43.0 %shard_map.113 = (f32[8,256]{1,0:T(8,128)}, bf16[128,256]{1,0:T(8,128)(2,1)}) custom-call(bf16[1,2,128,256]{3,2,1,0:T(8,128)(2,1)} %feat_hbm.1, bf16[9,3,256,256]{3,2,1,0:T(8,128)(2,1)} %bitcast.4, f32[8,256]{1,0:T(8,128)} %queries_hbm.1, bf16[2,256,256]{2,1,0:T(8,128)(2,1)} %wq_hbm.1, bf16[2,256,256]{2,1,0:T(8,128)(2,1)} %wk_hbm.1, ...), custom_call_target="tpu_custom_call" | custom-call | tf_op jit(solution)/shard_map/pallas_call | solution.py:425
  43.7 1.5 %reshape.15 = bf16[128,1,2,128]{3,2,0,1:T(2,128)(2,1)} reshape(bf16[128,256]{1,0:T(8,128)(2,1)} %get-tuple-element.5) | data formatting | bytes 131072 | tf_op jit(solution)/shard_map/reshape | solution.py:487
  45.2 1.3 %copy.14 = f32[8,256]{1,0:T(8,128)} copy(f32[8,256]{1,0:T(8,128)} %get-tuple-element.10) | data formatting | bytes 16384

commit v5 on v4

--- a/solution.py
+++ b/solution.py
@@ -470,19 +470,24 @@
             pltpu.SemaphoreType.REGULAR((2, 2)),
         ],
         compiler_params=pltpu.CompilerParams(
-            collective_id=0, has_side_effects=True, vmem_limit_bytes=60 * 1024 * 1024
+            collective_id=0, has_side_effects=True, vmem_limit_bytes=40 * 1024 * 1024
         ),
     )(
-        features,
-        conv_weight.reshape(9, 3, D, D),
-        queries,
-        w_query,
-        w_key,
-        w_value,
-        w_out,
-        norm_gain.reshape(1, D),
-        mask_weight,
-        mask_blocks.T,
+        *(
+            pltpu.with_memory_space_constraint(operand, pltpu.HBM)
+            for operand in (
+                features,
+                conv_weight.reshape(9, 3, D, D),
+                queries,
+                w_query,
+                w_key,
+                w_value,
+                w_out,
+                norm_gain.reshape(1, D),
+                mask_weight,
+                mask_blocks.T,
+            )
+        )
     )
     return embed, logits.reshape(NQ, 1, 2, NX)
 

time: 46.6 us -> 44.2 us (0.948)
  local copies, waits for them, and re-layouts: 2.78 us -> 1.25 us
  Pallas kernels: 43 us -> 42.2 us
    reshape x1, local copies, waits for them, and re-layouts: 1.49 us -> 0.65 us  [local(): return (embed, logits.reshape(NQ, 1, 2, NX))]
    pallas_call x1, Pallas kernels: 43 us -> 42.2 us  [local(): pl.pallas_call(kernel, out_shape=(jax.ShapeDtypeStruct((8, D), F32), jax....]
    unnamed x1, local copies, waits for them, and re-layouts: 1.29 us -> 0.6 us
where the time goes in v5:
time: 44.2 us; the launch traced here: 44.1 us
  Pallas kernels  42.2 us (95%)
  local copies, waits for them, and re-layouts  1.25 us (3%)
  between operations  0.64 us (1%)
    pallas_call x1, Pallas kernels, local(): pl.pallas_call(kernel, out_shape=(jax.ShapeDtypeStruct((8, D), F32), jax....  42.2 us

profile of v5, /device:TPU:1, one launch (start us, length us, event | category | flops | bytes accessed | tf_op | source)
XLA Modules:
  0.0 44.1 jit_solution(16506557652805994200)
XLA Ops:
  0.6 42.2 %shard_map.113 = (f32[8,256]{1,0:T(8,128)S(1)}, bf16[128,256]{1,0:T(8,128)(2,1)S(1)}) custom-call(bf16[1,2,128,256]{3,2,1,0:T(8,128)(2,1)} %feat_hbm.1, bf16[9,3,256,256]{3,2,1,0:T(8,128)(2,1)} %bitcast.4, f32[8,256]{1,0:T(8,128)} %queries_hbm.1, bf16[2,256,256]{2,1,0:T(8,128)(2,1)} %wq_hbm.1, bf16[2,256,256]{2,1,0:T(8,128)(2,1)} %wk_hbm.1, ...), custom_call_target="tpu_custom_call" | custom-call | tf_op jit(solution)/shard_map/pallas_call | solution.py:425
  42.8 0.7 %reshape.15 = bf16[128,1,2,128]{3,2,0,1:T(2,128)(2,1)} reshape(bf16[128,256]{1,0:T(8,128)(2,1)S(1)} %get-tuple-element.5) | data formatting | bytes 131072 | tf_op jit(solution)/shard_map/reshape | solution.py:492
  43.5 0.6 %copy.14 = f32[8,256]{1,0:T(8,128)} copy(f32[8,256]{1,0:T(8,128)S(1)} %get-tuple-element.10) | data formatting | bytes 16384

commit v6 on v5

--- a/solution.py
+++ b/solution.py
@@ -21,8 +21,8 @@
 ZS = 8
 CHUNKS = 4
 Z_ORDER = (0, 1, 7, 2, 6, 3, 5, 4)
-GROUPS = ((0, 8), (8, 14), (14, 16))
-PLACE_GROUP = (0, 0, 0, 0, 1, 1, 1, 2)
+GROUPS = ((0, 6), (6, 10), (10, 14), (14, 16))
+PLACE_GROUP = (0, 0, 0, 1, 1, 2, 2, 3)
 Z_SENDS = (4, 3, 5, 2, 6, 1, 7)
 XY_SENDS = sorted(
     ((dy, dx) for dy in range(4) for dx in range(4) if dy or dx),
@@ -54,28 +54,37 @@
     return ((z + offset) % ZS) * 2 + slot % 2
 
 
-def merge(ids, near, mid, far, pair_id, term_y, lane_z):
-    rows = ids.shape[0]
-    flat = far.reshape(QRY * 16, 128)
-    raised = pltpu.roll(flat.astype(F32), QRY * 16 - 4, axis=0).astype(BF16)
-    outs = jnp.concatenate(
-        [
-            jnp.concatenate([near[half].reshape(QRY * 16, 128) for half in range(2)], axis=1),
-            jnp.concatenate(
-                [mid[:, half * 16 : half * 16 + 16, :].reshape(QRY * 16, 128) for half in range(2)],
-                axis=1,
-            ),
-            jnp.concatenate([flat, raised], axis=1),
-        ],
-        axis=0,
-    )
+def choices(ids, pair_id, term_y):
     pick, term = [], []
     for j in range(MB):
         idj = ids[:, j : j + 1]
         pick.append(jnp.where(pair_id == idj, 1.0, 0.0).astype(BF16))
         term.append(jnp.where(term_y == idj % NY, 1.0, 0.0).astype(BF16))
-    lse = dot(jnp.concatenate(term, axis=0), flat)
-    chosen = dot(jnp.concatenate(pick, axis=0), outs)
+    return jnp.concatenate(pick, axis=0), jnp.concatenate(term, axis=0)
+
+
+def both_halves(block, rows):
+    flat = block.reshape(QRY * 16, 128)
+    raised = pltpu.roll(flat.astype(F32), QRY * 16 - rows, axis=0).astype(BF16)
+    return jnp.concatenate([flat, raised], axis=1)
+
+
+def choose_early(pick, near, mid):
+    outs = jnp.concatenate(
+        [
+            both_halves(mid[0], 8),
+            both_halves(mid[1], 8),
+            jnp.concatenate([near[half].reshape(QRY * 16, 128) for half in range(2)], axis=1),
+        ],
+        axis=0,
+    )
+    return dot(pick, outs)
+
+
+def merge(ids, chosen, pick, term, far, lane_z):
+    rows = ids.shape[0]
+    lse = dot(term, far.reshape(QRY * 16, 128))
+    chosen = chosen + dot(pick, both_halves(far, 4))
     lses = []
     for j in range(MB):
         lj = jnp.where(lane_z == ids[:, j : j + 1] // NY, lse[j * rows : (j + 1) * rows], 0.0)
@@ -95,8 +104,8 @@
 def kernel(
     feat_hbm, conv_hbm, queries_hbm, wq_hbm, wk_hbm, wv_hbm, wo_hbm, gain_hbm, mw_hbm, mb_hbm,
     embed_ref, logit_ref,
-    ext, taps, qbuf, qpbuf, wq, wk, wv, wo, mw, gain, mb, wvp, wop, pix, keys, vals,
-    stage1, near, mid, far, state, acc,
+    ext, taps, qbuf, qpbuf, wq, wk, wv, wo, mw, gain, mb, wvp, wop, pix, pix_t, keys, vals,
+    stage1, near, mid, far, state, acc, pick_all, term_all, woven,
     local_sem, conv_sem, halo_send, halo_recv, q_send, q_recv, p_send, p_recv,
     s_send, s_recv, y_send, y_recv, c_send, c_recv, entered,
 ):
@@ -111,14 +120,14 @@
     xy_index = [lax.rem(y + dy, 4) * 4 + lax.rem(x + dx, 4) for dy, dx in XY_SENDS]
 
     barrier = pltpu.get_barrier_semaphore()
-    for d in (1, -1, 2, -2):
+    for d in (1, -1, 2, -2, 3, -3, 4, -4):
         pl.semaphore_signal(barrier, inc=1, device_id=(wrap(s + d, SPAN), q), device_id_type=MESH)
     for block in xy_index[::-1]:
         pl.semaphore_signal(barrier, inc=1, device_id=(s, block), device_id_type=MESH)
 
     own = pltpu.make_async_copy(feat_hbm.at[0], ext.at[1, pl.ds(1, 2)], local_sem.at[0])
     own.start()
-    early, loads = [], []
+    first_loads, loads = [], []
     for k, (src, dst) in enumerate(
         (
             (mb_hbm, mb),
@@ -133,23 +142,16 @@
     ):
         copy = pltpu.make_async_copy(src, dst, local_sem.at[1 + k])
         copy.start()
-        (early if k < 3 else loads).append(copy)
+        (first_loads if k < 3 else loads).append(copy)
     conv_loads = [
         pltpu.make_async_copy(conv_hbm.at[:, dx], taps.at[dx], conv_sem.at[dx]) for dx in range(3)
     ]
     for load in conv_loads:
         load.start()
-    pl.semaphore_wait(barrier, 4 + len(xy_index))
-
-    def tell(step):
-        for k, d in enumerate((2 * step, -2 * step)):
-            pl.semaphore_signal(
-                entered.at[step - 1, k], inc=1, device_id=(wrap(s + d, SPAN), q), device_id_type=MESH
-            )
-
-    def hear(step):
-        for k in range(2):
-            pl.semaphore_wait(entered.at[step - 1, k], 1)
+    pl.semaphore_wait(barrier, 8 + len(xy_index))
+
+    for k, d in enumerate((4, -4)):
+        pl.semaphore_signal(entered.at[k], inc=1, device_id=(wrap(s + d, SPAN), q), device_id_type=MESH)
 
     sends = []
 
@@ -171,8 +173,6 @@
     from_down = send(rows, ext.at[0, pl.ds(1, 2)], 2 * CHUNKS, (up, q))
     from_up = send(rows, ext.at[2, pl.ds(1, 2)], 2 * CHUNKS + 1, (down, q))
 
-    tell(1)
-
     def to_plane(buf, send_sem, recv_sem):
         for block in xy_index:
             pltpu.make_async_remote_copy(
@@ -184,7 +184,7 @@
         some = buf.at[pl.ds(0, count)]
         pltpu.make_async_copy(some, some, sem).wait()
 
-    for load in early:
+    for load in first_loads:
         load.wait()
     qproj = (dot(qbuf[q].astype(BF16), wq[0]) * HEAD_DIM**-0.5).astype(BF16)
     qpbuf[q] = jnp.concatenate([qproj[:, 0:128], qproj[:, 128:256]], axis=0)
@@ -213,18 +213,21 @@
     own_ids = jnp.concatenate(own_ids + [jnp.full((6, MB), -1.0, F32)], axis=0).astype(jnp.int32)
     picks = jnp.concatenate(picks + [jnp.zeros((6, NQ), F32)], axis=0).astype(BF16)
 
-    col = iota((1, QRY * 48), 1)
+    col = iota((1, QRY * 64), 1)
     group, kind = col // 256, col % 16
-    slot = jnp.where(group < 2, group * 8 + col % 8, 14 + col % 2)
-    half = jnp.where(group < 2, kind // 8, kind // 2)
-    limit = jnp.where(group == 0, 8, jnp.where(group == 1, 6, 4))
-    pair_id = slot_plane(slot, z) * NY + ((col % 256) // 16) * 2 + half
-    pair_id = jnp.where(jnp.where(group < 2, col % 8, kind) < limit, pair_id, -2)
+    group = jnp.where(group == 3, 3, jnp.where(group == 2, 0, group + 1))
+    width = jnp.where(group == 0, 8, jnp.where(group == 3, 2, 4))
+    place = kind & (width - 1)
+    half = (kind - place) // width
+    pair_id = slot_plane(jnp.where(group == 0, 0, 2 + 4 * group) + place, z) * NY + ((col % 256) // 16) * 2 + half
+    valid = jnp.where(half < 2, place, 8) < jnp.where(group == 0, 6, width)
+    pair_id = jnp.where(valid, pair_id, -2)
     row = iota((1, QRY * 16), 1)
     kind = row % 16 - 8
     term_y = (row // 16) * 2 + jnp.where(kind < 3, 0, 1)
     term_y = jnp.where((kind >= 0) & (kind < 6), term_y, -2)
     lane_z = slot_plane(iota((1, 128), 1) // HEADS, z)
+    own_pick, own_term = choices(own_ids, pair_id, term_y)
 
     relays = []
     for k, copy in enumerate(across):
@@ -233,8 +236,6 @@
         first = 2 * CHUNKS + 2 + 2 * k
         relays.append(send(ext.at[1, row, chunk], ext.at[0, row, chunk], first, (up, q)))
         relays.append(send(ext.at[1, row, chunk], ext.at[2, row, chunk], first + 1, (down, q)))
-    hear(1)
-    tell(2)
     own.wait()
     for load in conv_loads:
         load.wait()
@@ -305,12 +306,13 @@
     head_of = iota((HEADS, D), 1) // HEAD_DIM == iota((HEADS, D), 0)
     head_of_lane = iota((HEADS, D), 1) % HEADS == iota((HEADS, D), 0)
     lse_lane = iota((HEADS, 128), 1) % HEADS == iota((HEADS, 128), 0)
-    hear(2)
+    for k in range(2):
+        pl.semaphore_wait(entered.at[k], 1)
     for layer in range(LAYERS):
         spread = jnp.concatenate(
             [jnp.where(head_of, qproj[r : r + 1], 0.0) for r in range(2)], axis=0
         ).astype(BF16)
-        scores = dot_nt(spread, keys[layer])
+        scores = dot_nt(spread, keys[0]) if layer == 0 else dot(spread, keys[1])
         scores = jnp.concatenate([scores[0:8, 0:NX], scores[8:16, NX : 2 * NX]], axis=0)
         top = jnp.max(scores, axis=1, keepdims=True)
         prob = jnp.exp(scores - top)
@@ -337,10 +339,13 @@
             ).start()
         if layer == 0:
             to_plane(qbuf, q_send, q_recv)
-            keys[1] = dot(pix[...], wk[1]).astype(BF16)
+            keys[1] = dot(pix[...], wk[1]).T.astype(BF16)
+            pix_t[...] = pix[...].astype(F32).T.astype(BF16)
             vals[1] = dot(pix[...], wvp[1]).astype(BF16)
+            pick_all[...], term_all[...] = choices(all_ids, pair_id, term_y)
         else:
-            attn = merge(all_ids, near[0], mid[0], far[0], pair_id, term_y, lane_z)
+            chosen = choose_early(pick_all[:, : QRY * 48], near[0], mid[0])
+            attn = merge(all_ids, chosen, pick_all[:, QRY * 48 :], term_all[...], far[0], lane_z)
             state[...] = qbuf[...].reshape(NQ, D) + dot(attn.astype(BF16), wop[0])
         lines = [jnp.zeros((1, 128), F32)] * 2
         for group, (start, end) in enumerate(GROUPS):
@@ -353,14 +358,15 @@
                 kept = jnp.where(own_lanes, got[:, 4 + r, :], 0.0)
                 lines[r] = lines[r] + jnp.sum(kept, axis=0, keepdims=True)
             if group == 0:
-                halves = [jnp.concatenate(parts[2 * k : 2 * k + 2], axis=0) for k in range(2)]
+                blank = jnp.zeros((2, 128), F32)
+                halves = [
+                    jnp.concatenate([parts[2 * k], blank, parts[2 * k + 1], blank], axis=0) for k in range(2)
+                ]
                 near[layer, core, q] = jnp.where(core == 0, halves[0], halves[1]).astype(BF16)
                 to_plane(near.at[layer, core], y_send.at[layer, 0], y_recv.at[layer, 0])
-            elif group == 1:
-                blank = jnp.zeros((2, 128), F32)
-                message = [piece for part in parts for piece in (part, blank)]
-                mid[layer, q] = jnp.concatenate(message, axis=0).astype(BF16)
-                to_plane(mid.at[layer], y_send.at[layer, 1], y_recv.at[layer, 1])
+            elif group < 3:
+                mid[layer, group - 1, q] = jnp.concatenate(parts, axis=0).astype(BF16)
+                to_plane(mid.at[layer, group - 1], y_send.at[layer, group], y_recv.at[layer, group])
         message = parts
         for line in lines:
             for _ in range(3):
@@ -369,7 +375,7 @@
                 line = line - term
         message.append(jnp.zeros((2, 128), F32))
         far[layer, q] = jnp.concatenate(message, axis=0).astype(BF16)
-        to_plane(far.at[layer], y_send.at[layer, 2], y_recv.at[layer, 2])
+        to_plane(far.at[layer], y_send.at[layer, 3], y_recv.at[layer, 3])
         if layer == 0:
             wait_slots(qbuf, QRY - 1, q_recv)
             state_all = qbuf[...].reshape(NQ, D)
@@ -385,15 +391,18 @@
         )
         swap.start()
         sends.append(swap)
-        wait_slots(mid.at[layer], QRY - 1, y_recv.at[layer, 1])
-        wait_slots(far.at[layer], QRY - 1, y_recv.at[layer, 2])
+        for k in range(2):
+            wait_slots(mid.at[layer, k], QRY - 1, y_recv.at[layer, 1 + k])
         swap.wait_recv()
+        early = own_pick[:, : QRY * 48] if layer == 0 else pick_all[:, : QRY * 48]
+        chosen = choose_early(early, near[layer], mid[layer])
+        wait_slots(far.at[layer], QRY - 1, y_recv.at[layer, 3])
         if layer == 0:
-            attn = merge(own_ids, near[0], mid[0], far[0], pair_id, term_y, lane_z)
+            attn = merge(own_ids, chosen, own_pick[:, QRY * 48 :], own_term, far[0], lane_z)
             own_state = own_state + dot(attn.astype(BF16), wop[0])
             qproj = (dot(own_state.astype(BF16), wq[1]) * HEAD_DIM**-0.5).astype(BF16).astype(F32)
 
-    attn = merge(all_ids, near[1], mid[1], far[1], pair_id, term_y, lane_z)
+    attn = merge(all_ids, chosen, pick_all[:, QRY * 48 :], term_all[...], far[1], lane_z)
     final = state[...] + dot(attn.astype(BF16), wop[1])
     mean = jnp.mean(final, axis=-1, keepdims=True)
     centered = final - mean
@@ -402,7 +411,10 @@
     state[...] = embed
     embed_ref[...] = state[pl.ds(pl.multiple_of(q * 8, 8), 8), :]
     mask_embed = dot(embed.astype(BF16), mw[...]).astype(BF16)
-    logit_ref[...] = (dot_nt(mask_embed, pix[...]) * D**-0.5).astype(BF16)
+    logits = dot(mask_embed, pix_t[...]) * D**-0.5
+    for r in range(2):
+        woven[pl.ds(r, NQ, stride=2), :] = logits[:, r * NX : (r + 1) * NX]
+    logit_ref[...] = woven[...].astype(BF16)
 
     for copy in sends:
         copy.wait_send()
@@ -411,8 +423,20 @@
     for layer in range(LAYERS):
         wait_slots(stage1.at[layer], SPAN - 1, s_send.at[layer])
         wait_slots(near.at[layer, 0], QRY - 1, y_send.at[layer, 0])
-        wait_slots(mid.at[layer], QRY - 1, y_send.at[layer, 1])
-        wait_slots(far.at[layer], QRY - 1, y_send.at[layer, 2])
+        for k in range(2):
+            wait_slots(mid.at[layer, k], QRY - 1, y_send.at[layer, 1 + k])
+        wait_slots(far.at[layer], QRY - 1, y_send.at[layer, 3])
+
+
+def hand_over(embed_ref, logit_ref, embed_out, logit_out, sem):
+    copies = [
+        pltpu.make_async_copy(logit_ref, logit_out, sem.at[0]),
+        pltpu.make_async_copy(embed_ref, embed_out, sem.at[1]),
+    ]
+    for copy in copies:
+        copy.start()
+    for copy in copies:
+        copy.wait()
 
 
 def local(
@@ -426,7 +450,7 @@
         kernel,
         out_shape=(
             jax.ShapeDtypeStruct((8, D), F32),
-            jax.ShapeDtypeStruct((NQ, 2 * NX), BF16),
+            jax.ShapeDtypeStruct((2 * NQ, NX), BF16),
         ),
         in_specs=[hbm] * 10,
         out_specs=(vmem, vmem),
@@ -445,14 +469,18 @@
             square,
             square,
             pltpu.VMEM((2 * NX, D), BF16),
+            pltpu.VMEM((D, 2 * NX), BF16),
             square,
             square,
             pltpu.VMEM((LAYERS, SPAN, 8, 128), F32),
             pltpu.VMEM((LAYERS, 2, QRY, 16, 128), BF16),
-            pltpu.VMEM((LAYERS, QRY, 32, 128), BF16),
+            pltpu.VMEM((LAYERS, 2, QRY, 16, 128), BF16),
             pltpu.VMEM((LAYERS, QRY, 16, 128), BF16),
             pltpu.VMEM((NQ, D), F32),
             pltpu.VMEM((3, 2 * NX, D), F32),
+            pltpu.VMEM((MB * NQ, QRY * 64), BF16),
+            pltpu.VMEM((MB * NQ, QRY * 16), BF16),
+            pltpu.VMEM((2 * NQ, NX), F32),
             dma((9,)),
             dma((3,)),
             dma((6 * CHUNKS + 2,)),
@@ -462,12 +490,12 @@
             dma,
             dma,
             dma((LAYERS,)),
-            dma((LAYERS, 3)),
-            dma((LAYERS, 3)),
-            dma((LAYERS, 3)),
+            dma((LAYERS, 4)),
+            dma((LAYERS, 4)),
+            dma((LAYERS, 4)),
             dma((LAYERS,)),
             dma((LAYERS,)),
-            pltpu.SemaphoreType.REGULAR((2, 2)),
+            pltpu.SemaphoreType.REGULAR((2,)),
         ],
         compiler_params=pltpu.CompilerParams(
             collective_id=0, has_side_effects=True, vmem_limit_bytes=40 * 1024 * 1024
@@ -489,6 +517,16 @@
             )
         )
     )
+    embed, logits = pl.pallas_call(
+        hand_over,
+        out_shape=(
+            jax.ShapeDtypeStruct((8, D), F32),
+            jax.ShapeDtypeStruct((2 * NQ, NX), BF16),
+        ),
+        in_specs=[vmem] * 2,
+        out_specs=(pl.BlockSpec(memory_space=pl.ANY),) * 2,
+        scratch_shapes=[dma((2,))],
+    )(*(pltpu.with_memory_space_constraint(part, pltpu.VMEM) for part in (embed, logits)))
     return embed, logits.reshape(NQ, 1, 2, NX)
 
 

time: 44.2 us -> 43.5 us (0.984)
  local copies, waits for them, and re-layouts: 1.25 us -> 0 us
  Pallas kernels: 42.2 us -> 42.7 us
    pallas_call x0 -> x1, Pallas kernels: none -> 0.65 us  [local(): pl.pallas_call(hand_over, out_shape=(jax.ShapeDtypeStruct((8, D), F32), j...]
    reshape x1 -> x0, local copies, waits for them, and re-layouts: 0.65 us -> none  [local(): return (embed, logits.reshape(NQ, 1, 2, NX))]
    unnamed x1 -> x0, local copies, waits for them, and re-layouts: 0.6 us -> none
where the time goes in v6:
time: 43.5 us; the launch traced here: 43.4 us
  Pallas kernels  42.7 us (98%)
  between operations  0.64 us (1%)
    pallas_call x1, Pallas kernels, local(): pl.pallas_call(kernel, out_shape=(jax.ShapeDtypeStruct((8, D), F32), jax....  42.1 us

profile of v6, /device:TPU:1, one launch (start us, length us, event | category | flops | bytes accessed | tf_op | source)
XLA Modules:
  0.0 43.4 jit_solution(10566527847139612518)
XLA Ops:
  0.6 42.1 %shard_map.113 = (f32[8,256]{1,0:T(8,128)S(1)}, bf16[256,128]{1,0:T(8,128)(2,1)S(1)}) custom-call(bf16[1,2,128,256]{3,2,1,0:T(8,128)(2,1)} %feat_hbm.1, bf16[9,3,256,256]{3,2,1,0:T(8,128)(2,1)} %bitcast.6, f32[8,256]{1,0:T(8,128)} %queries_hbm.1, bf16[2,256,256]{2,1,0:T(8,128)(2,1)} %wq_hbm.1, bf16[2,256,256]{2,1,0:T(8,128)(2,1)} %wk_hbm.1, ...), custom_call_target="tpu_custom_call" | custom-call | tf_op jit(solution)/shard_map/pallas_call | solution.py:449
  42.7 0.7 %shard_map.114 = (f32[8,256]{1,0:T(8,128)}, bf16[256,128]{1,0:T(8,128)(2,1)}) custom-call(f32[8,256]{1,0:T(8,128)S(1)} %get-tuple-element.6.embed_ref, bf16[256,128]{1,0:T(8,128)(2,1)S(1)} %get-tuple-element.7.logit_ref), custom_call_target="tpu_custom_call" | custom-call | tf_op jit(solution)/shard_map/pallas_call | solution.py:520

commit v7 on v6

--- a/solution.py
+++ b/solution.py
@@ -228,6 +228,7 @@
     term_y = jnp.where((kind >= 0) & (kind < 6), term_y, -2)
     lane_z = slot_plane(iota((1, 128), 1) // HEADS, z)
     own_pick, own_term = choices(own_ids, pair_id, term_y)
+    pick_all[...], term_all[...] = choices(all_ids, pair_id, term_y)
 
     relays = []
     for k, copy in enumerate(across):
@@ -236,6 +237,7 @@
         first = 2 * CHUNKS + 2 + 2 * k
         relays.append(send(ext.at[1, row, chunk], ext.at[0, row, chunk], first, (up, q)))
         relays.append(send(ext.at[1, row, chunk], ext.at[2, row, chunk], first + 1, (down, q)))
+    to_plane(qbuf, q_send, q_recv)
     own.wait()
     for load in conv_loads:
         load.wait()
@@ -338,15 +340,9 @@
                 device_id=(plane, q), device_id_type=MESH,
             ).start()
         if layer == 0:
-            to_plane(qbuf, q_send, q_recv)
             keys[1] = dot(pix[...], wk[1]).T.astype(BF16)
             pix_t[...] = pix[...].astype(F32).T.astype(BF16)
             vals[1] = dot(pix[...], wvp[1]).astype(BF16)
-            pick_all[...], term_all[...] = choices(all_ids, pair_id, term_y)
-        else:
-            chosen = choose_early(pick_all[:, : QRY * 48], near[0], mid[0])
-            attn = merge(all_ids, chosen, pick_all[:, QRY * 48 :], term_all[...], far[0], lane_z)
-            state[...] = qbuf[...].reshape(NQ, D) + dot(attn.astype(BF16), wop[0])
         lines = [jnp.zeros((1, 128), F32)] * 2
         for group, (start, end) in enumerate(GROUPS):
             count = end - start
@@ -376,6 +372,10 @@
         message.append(jnp.zeros((2, 128), F32))
         far[layer, q] = jnp.concatenate(message, axis=0).astype(BF16)
         to_plane(far.at[layer], y_send.at[layer, 3], y_recv.at[layer, 3])
+        if layer == 1:
+            chosen = choose_early(pick_all[:, : QRY * 48], near[0], mid[0])
+            attn = merge(all_ids, chosen, pick_all[:, QRY * 48 :], term_all[...], far[0], lane_z)
+            state[...] = qbuf[...].reshape(NQ, D) + dot(attn.astype(BF16), wop[0])
         if layer == 0:
             wait_slots(qbuf, QRY - 1, q_recv)
             state_all = qbuf[...].reshape(NQ, D)

time: 43.5 us -> 43.4 us (level)
  no operation moved by 1% of the time
where the time goes in v7:
time: 43.4 us; the launch traced here: 43.3 us
  Pallas kernels  42.7 us (98%)
  between operations  0.64 us (1%)
    pallas_call x1, Pallas kernels, local(): pl.pallas_call(kernel, out_shape=(jax.ShapeDtypeStruct((8, D), F32), jax....  42.1 us

profile of v7, /device:TPU:1, one launch (start us, length us, event | category | flops | bytes accessed | tf_op | source)
XLA Modules:
  0.0 43.3 jit_solution(5785830548303203886)
XLA Ops:
  0.6 42.1 %shard_map.113 = (f32[8,256]{1,0:T(8,128)S(1)}, bf16[256,128]{1,0:T(8,128)(2,1)S(1)}) custom-call(bf16[1,2,128,256]{3,2,1,0:T(8,128)(2,1)} %feat_hbm.1, bf16[9,3,256,256]{3,2,1,0:T(8,128)(2,1)} %bitcast.6, f32[8,256]{1,0:T(8,128)} %queries_hbm.1, bf16[2,256,256]{2,1,0:T(8,128)(2,1)} %wq_hbm.1, bf16[2,256,256]{2,1,0:T(8,128)(2,1)} %wk_hbm.1, ...), custom_call_target="tpu_custom_call" | custom-call | tf_op jit(solution)/shard_map/pallas_call | solution.py:449
  42.7 0.7 %shard_map.114 = (f32[8,256]{1,0:T(8,128)}, bf16[256,128]{1,0:T(8,128)(2,1)}) custom-call(f32[8,256]{1,0:T(8,128)S(1)} %get-tuple-element.6.embed_ref, bf16[256,128]{1,0:T(8,128)(2,1)S(1)} %get-tuple-element.7.logit_ref), custom_call_target="tpu_custom_call" | custom-call | tf_op jit(solution)/shard_map/pallas_call | solution.py:520

commit v8 on v6

--- a/solution.py
+++ b/solution.py
@@ -26,7 +26,7 @@
 Z_SENDS = (4, 3, 5, 2, 6, 1, 7)
 XY_SENDS = sorted(
     ((dy, dx) for dy in range(4) for dx in range(4) if dy or dx),
-    key=lambda t: -(min(t[0], 4 - t[0]) + min(t[1], 4 - t[1])),
+    key=lambda t: -(min(t[0], 4 - t[0]) * 10 + min(t[1], 4 - t[1]) * 11),
 )
 
 

time: 43.5 us -> 43.5 us (level)
  no operation moved by 1% of the time
where the time goes in v8:
time: 43.5 us; the launch traced here: 43.4 us
  Pallas kernels  42.7 us (98%)
  between operations  0.64 us (1%)
    pallas_call x1, Pallas kernels, local(): pl.pallas_call(kernel, out_shape=(jax.ShapeDtypeStruct((8, D), F32), jax....  42.1 us

profile of v8, /device:TPU:1, one launch (start us, length us, event | category | flops | bytes accessed | tf_op | source)
XLA Modules:
  0.0 43.4 jit_solution(3425771229158622936)
XLA Ops:
  0.6 42.1 %shard_map.113 = (f32[8,256]{1,0:T(8,128)S(1)}, bf16[256,128]{1,0:T(8,128)(2,1)S(1)}) custom-call(bf16[1,2,128,256]{3,2,1,0:T(8,128)(2,1)} %feat_hbm.1, bf16[9,3,256,256]{3,2,1,0:T(8,128)(2,1)} %bitcast.6, f32[8,256]{1,0:T(8,128)} %queries_hbm.1, bf16[2,256,256]{2,1,0:T(8,128)(2,1)} %wq_hbm.1, bf16[2,256,256]{2,1,0:T(8,128)(2,1)} %wk_hbm.1, ...), custom_call_target="tpu_custom_call" | custom-call | tf_op jit(solution)/shard_map/pallas_call | solution.py:449
  42.7 0.7 %shard_map.114 = (f32[8,256]{1,0:T(8,128)}, bf16[256,128]{1,0:T(8,128)(2,1)}) custom-call(f32[8,256]{1,0:T(8,128)S(1)} %get-tuple-element.6.embed_ref, bf16[256,128]{1,0:T(8,128)(2,1)S(1)} %get-tuple-element.7.logit_ref), custom_call_target="tpu_custom_call" | custom-call | tf_op jit(solution)/shard_map/pallas_call | solution.py:520
